TPU v7x, 128 devices: a whole 4x4x4 slice. The times are simulated.
128 devices in a mesh: row: 8 (over y_hi, x), col: 16 (over z, y_lo, core).
Axes of the slice: x: 4, y: 4 (y_hi: 2, y_lo: 2; y = y_hi * 2 + y_lo), z: 4, core: 2. Of those that a mesh axis runs over, the one named last changes fastest.
Arguments:
- acts: bfloat16 [2048, 8192], P('row', 'col'), may hold values from -6 to 6
- grads: bfloat16 [2048, 8192], P('col', 'row'), may hold values from -6 to 6
- basis_acts: bfloat16 [8192, 8192], P('col', 'row'), may hold values from -0.0625 to 0.0625
- basis_grads: bfloat16 [8192, 8192], P('row', 'col'), may hold values from -0.0625 to 0.0625
Outputs:
- correction: float32 [8192, 8192], P('col', 'row')
All inputs are finite; a program needn't handle non-finite values.
Results may differ from a plain program's by a relative error of at most 0.0041.
Values may be sent and summed in bfloat16 or wider, within the bound.
A program may use at most 64 MiB of HBM per device.

v0:
```python
import jax
import jax.numpy as jnp
from jax import lax
from jax.sharding import PartitionSpec as P

SEQS = 2


def on_device(acts, grads, basis_acts, basis_grads):
    acts_full = lax.all_gather(acts, "row", axis=0, tiled=True)
    grads_full = lax.all_gather(grads, "col", axis=0, tiled=True)
    rows_part = acts_full
    act_share = lax.psum_scatter(
        jnp.dot(rows_part, basis_acts, preferred_element_type=jnp.float32),
        "col",
        scatter_dimension=0,
        tiled=True,
    )
    rotated_acts = lax.all_gather(act_share.astype(jnp.bfloat16), "col", axis=0, tiled=True)
    rows_part = grads_full
    grad_share = lax.psum_scatter(
        jnp.dot(rows_part, basis_grads, preferred_element_type=jnp.float32),
        "row",
        scatter_dimension=0,
        tiled=True,
    )
    rotated_grads = lax.all_gather(grad_share.astype(jnp.bfloat16), "row", axis=0, tiled=True)
    seq_len = rotated_acts.shape[0] // SEQS
    grad_seqs = rotated_grads.reshape(SEQS, seq_len, rotated_grads.shape[1])
    act_seqs = rotated_acts.reshape(SEQS, seq_len, rotated_acts.shape[1])
    blocks = jnp.einsum("sti,stj->sij", grad_seqs, act_seqs, preferred_element_type=jnp.float32)
    return jnp.sum(blocks * blocks, axis=0) / (SEQS * seq_len)


def solution(mesh):
    return jax.shard_map(
        on_device,
        mesh=mesh,
        in_specs=(P("row", "col"), P("col", "row"), P("col", "row"), P("row", "col")),
        out_specs=P("col", "row"),
        check_vma=False,
    )
```

profile of v0, /device:TPU:1, one launch (start us, length us, event | category | flops | bytes accessed | tf_op | source)
XLA Modules:
  0.0 401.5 jit_solution(13539106658459933371)
XLA Ops:
  6.5 0.7 all-gather.5.cloned.1.call-update
  7.3 0.0 all-gather.9.cloned.1.call-start
  7.3 0.7 all-gather.9.cloned.1.call-update
  8.0 0.0 reduce-scatter.3.cloned.1.call-start
  8.1 42.1 %all-gather.5.cloned.1.call-done = bf16[2048,1024]{1,0:T(8,128)(2,1)} async-done(((bf16[128,1024]{1,0:T(8,128)(2,1)}), bf16[2048,1024]{1,0:T(8,128)(2,1)}) %all-gather.5.cloned.1.call-update) | async-done | bytes 4194320 | tf_op jit(solution)/shard_map/all_gather | solution.py:11
  50.2 6.8 %fusion = f32[2048,512]{1,0:T(8,128)} fusion(bf16[2048,1024]{1,0:T(8,128)(2,1)} %all-gather.5.cloned.1.call-done, bf16[1024,512]{1,0:T(8,128)(2,1)} %param.7), kind=kOutput, calls=%fused_computation.2 | convolution fusion | flops 2147483648 | bytes 9437184 | tf_op jit(solution)/shard_map/dot_general | solution.py:22
  56.9 0.0 reduce-scatter.3.cloned.1.call-update
  57.0 0.0 reduce-scatter.5.cloned.1.call-start
  57.0 48.7 %all-gather.9.cloned.1.call-done = bf16[2048,512]{1,0:T(8,128)(2,1)} async-done(((bf16[256,512]{1,0:T(8,128)(2,1)}), bf16[2048,512]{1,0:T(8,128)(2,1)}) %all-gather.9.cloned.1.call-update) | async-done | bytes 2097168 | tf_op jit(solution)/shard_map/all_gather | solution.py:10
  105.7 0.0 copy-done
  105.7 7.2 %fusion.1 = f32[2048,1024]{1,0:T(8,128)} fusion(bf16[2048,512]{1,0:T(8,128)(2,1)} %all-gather.9.cloned.1.call-done, bf16[512,1024]{1,0:T(8,128)(2,1)S(1)} %copy-done), kind=kOutput, calls=%fused_computation.3 | convolution fusion | flops 2147483648 | bytes 11534336 | tf_op jit(solution)/shard_map/dot_general | solution.py:14
  112.8 0.0 reduce-scatter.5.cloned.1.call-update
  112.9 0.0 all-gather.7.cloned.1.call-start
  112.9 80.3 %reduce-scatter.3.cloned.1.call-done = f32[256,512]{1,0:T(8,128)} async-done(((f32[2048,512]{1,0:T(8,128)}), f32[256,512]{1,0:T(8,128)}) %reduce-scatter.3.cloned.1.call-update) | async-done | bytes 524304 | tf_op jit(solution)/shard_map/reduce_scatter | solution.py:21
  193.3 1.8 convert_element_type.6
  195.0 0.0 all-gather.7.cloned.1.call-update
  195.1 0.0 all-gather.11.cloned.1.call-start
  195.1 96.7 %reduce-scatter.5.cloned.1.call-done = f32[128,1024]{1,0:T(8,128)} async-done(((f32[2048,1024]{1,0:T(8,128)}), f32[128,1024]{1,0:T(8,128)}) %reduce-scatter.5.cloned.1.call-update) | async-done | bytes 524304 | tf_op jit(solution)/shard_map/reduce_scatter | solution.py:13
  291.8 1.8 convert_element_type.7
  293.6 0.0 all-gather.11.cloned.1.call-update
  293.6 54.4 %all-gather.7.cloned.1.call-done = bf16[2048,512]{1,0:T(8,128)(2,1)} async-done(((bf16[256,512]{1,0:T(8,128)(2,1)}), bf16[2048,512]{1,0:T(8,128)(2,1)}) %all-gather.7.cloned.1.call-update) | async-done | bytes 2097168 | tf_op jit(solution)/shard_map/all_gather | solution.py:27
  348.1 39.6 %all-gather.11.cloned.1.call-done = bf16[2048,1024]{1,0:T(8,128)(2,1)} async-done(((bf16[128,1024]{1,0:T(8,128)(2,1)}), bf16[2048,1024]{1,0:T(8,128)(2,1)}) %all-gather.11.cloned.1.call-update) | async-done | bytes 4194320 | tf_op jit(solution)/shard_map/all_gather | solution.py:19
  387.7 5.4 %multiply_reduce_fusion = f32[512,1024]{1,0:T(8,128)S(1)} fusion(bf16[2,1024,512]{2,1,0:T(8,128)(2,1)} %bitcast.9, bf16[2,1024,1024]{2,1,0:T(8,128)(2,1)} %bitcast.8), kind=kOutput, calls=%fused_computation | convolution fusion | flops 2149056512 | bytes 8388608 | tf_op jit(solution)/shard_map/sti,stj->sij/dot_general | solution.py:31
  393.1 1.6 broadcast_multiply_fusion
  (2 shorter events, 0.0 us)
Async XLA Ops:
  6.5 99.2 %copy-start = (bf16[512,1024]{1,0:T(8,128)(2,1)S(1)}, bf16[512,1024]{1,0:T(8,128)(2,1)}, u32[]{:S(2)}) copy-start(bf16[512,1024]{1,0:T(8,128)(2,1)} %param.6) | copy-start | bytes 3145732
  6.5 43.6 %all-gather.5.cloned.1.call-start = ((), (), s32[]{:S(2)}) async-start(), calls=%async_computation.2 | async-start | bytes 4456448 | tf_op jit(solution)/shard_map/all_gather | solution.py:11
  7.3 98.4 %all-gather.9.cloned.1.call-start = ((), (), s32[]{:S(2)}) async-start(), calls=%async_computation.5 | async-start | bytes 2359296 | tf_op jit(solution)/shard_map/all_gather | solution.py:10
  8.0 185.3 %reduce-scatter.3.cloned.1.call-start = ((), (), s32[]{:S(2)}) async-start(), calls=%async_computation.3 | async-start | bytes 4718592 | tf_op jit(solution)/shard_map/reduce_scatter | solution.py:21
  57.0 234.8 %reduce-scatter.5.cloned.1.call-start = ((), (), s32[]{:S(2)}) async-start(), calls=%async_computation.6 | async-start | bytes 8912896 | tf_op jit(solution)/shard_map/reduce_scatter | solution.py:13
  112.9 235.2 %all-gather.7.cloned.1.call-start = ((), (), s32[]{:S(2)}) async-start(), calls=%async_computation.4 | async-start | bytes 2359296 | tf_op jit(solution)/shard_map/all_gather | solution.py:27
  195.1 192.6 %all-gather.11.cloned.1.call-start = ((), (), s32[]{:S(2)}) async-start(), calls=%async_computation.7 | async-start | bytes 4456448 | tf_op jit(solution)/shard_map/all_gather | solution.py:19
Sparse Core Ops, SparseCore 0:
  9.1 41.0 all-gather.4
  52.5 53.1 all-gather.8
  109.6 83.6 reduce-scatter.2
  195.5 96.2 reduce-scatter.4
  294.0 54.0 all-gather.6
  349.6 37.9 all-gather.10
where the time goes:
time: 402 us
  waiting for transfers between devices  363 us (90%)
  matrix products  19.4 us (5%)
  between operations  13.5 us (3%)
  other arithmetic  5.15 us (1%)
    reduce_scatter x1, waiting for transfers between devices, on_device(): lax.psum_scatter(jnp.dot(rows_part, basis_acts, preferred_element_type=jn...  96.7 us
    reduce_scatter x1, waiting for transfers between devices, on_device(): lax.psum_scatter(jnp.dot(rows_part, basis_grads, preferred_element_type=j...  80.3 us
    all_gather x1, waiting for transfers between devices, on_device(): lax.all_gather(grad_share.astype(jnp.bfloat16), 'row', axis=0, tiled=True)  54.4 us
    all_gather x1, waiting for transfers between devices, on_device(): acts_full = lax.all_gather(acts, 'row', axis=0, tiled=True)  48.7 us
    all_gather x1, waiting for transfers between devices, on_device(): grads_full = lax.all_gather(grads, 'col', axis=0, tiled=True)  42.1 us
    all_gather x1, waiting for transfers between devices, on_device(): lax.all_gather(act_share.astype(jnp.bfloat16), 'col', axis=0, tiled=True)  39.6 us
  transfers between devices with their start and end apart: 6, of which 6 were waited for; matrix products, arithmetic and copies ran while one was open for 4% of the time, Pallas kernels for 0%

commit v1 on v0

v1 whole, which is shorter than its diff:
```python
import jax
import jax.numpy as jnp
from jax import lax
from jax.experimental import pallas as pl
from jax.experimental.pallas import tpu as pltpu
from jax.sharding import PartitionSpec as P

MESH = pl.DeviceIdType.MESH
F32, BF16 = jnp.float32, jnp.bfloat16

TOKENS, D, SEQS = 2048, 8192, 2
SHARDS = 8
HALF = TOKENS // SHARDS // 2
PIECE = HALF // SHARDS
WIDE = 1024
NARROW = WIDE // 2
GROUPS = 4
TILE = 256

UP = 2.0 ** 30


def encode(v):
    v = v * UP
    return (v * v * v).astype(BF16)


def decode(c):
    c = c.astype(F32)
    size = jnp.maximum(jnp.abs(c), 2.0 ** -126)
    return c * (jnp.exp2(jnp.log2(size) * (-2.0 / 3.0)) * (1.0 / UP))


class Chain:
    def __init__(self, **refs):
        self.__dict__.update(refs)
        self.copies = {}


def kernel(acts, grads, qa, qs, out,
           xa, xg, wa, wg, pa, pg, rot_a, rot_g, rot_ao, rot_go, gt,
           sp1a, sm1a, sp2a, sm2a, s3a, rp1a, rm1a, rp2a, rm2a, r3a,
           sp1g, sm1g, sp2g, sm2g, s3g, rp1g, rm1g, rp2g, rm2g, r3g,
           local_sem, send_sem, recv_sem):
    row, col = lax.axis_index("row"), lax.axis_index("col")
    yh, x = row // 4, row % 4
    z, yl, h = col // 4, (col // 2) % 2, col % 2

    def dev(yh, x, z, yl, h):
        return (yh * 4 + x, z * 4 + yl * 2 + h)

    x_plus, x_minus = dev(yh, (x + 1) % 4, z, yl, h), dev(yh, (x + 3) % 4, z, yl, h)
    z_plus, z_minus = dev(yh, x, (z + 1) % 4, yl, h), dev(yh, x, (z + 3) % 4, yl, h)
    y_far, y_near = dev(1 - yh, x, z, yl, h), dev(yh, x, z, 1 - yl, h)
    other = dev(yh, x, z, yl, 1 - h)

    barrier = pltpu.get_barrier_semaphore()
    neighbours = (x_plus, x_minus, z_plus, z_minus, y_far, y_near, other)
    for n in neighbours:
        pl.semaphore_signal(barrier, inc=1, device_id=n, device_id_type=MESH)

    sems = [0]
    started = []

    def send(chain, name, src, dst, to):
        i = sems[0]
        sems[0] += 1
        copy = pltpu.make_async_remote_copy(
            src_ref=src, dst_ref=dst, send_sem=send_sem.at[i], recv_sem=recv_sem.at[i],
            device_id=to, device_id_type=MESH)
        copy.start()
        started.append(copy)
        chain.copies[name] = copy

    def arrived(chain, *names):
        for name in names:
            chain.copies[name].wait_recv()

    def piece(q):
        return pl.ds(pl.multiple_of(q * PIECE, PIECE), PIECE)

    a = Chain(plus=x_plus, minus=x_minus, partner=y_far, sum_plus=z_plus, sum_minus=z_minus, sum_partner=y_near,
              q=lambda d, e: ((z + d) % 4) * 2 + (yl + e) % 2,
              x=xa, w=wa, p=pa, rot=rot_a, sp1=sp1a, sm1=sm1a, sp2=sp2a, sm2=sm2a, s3=s3a,
              rp1=rp1a, rm1=rm1a, rp2=rp2a, rm2=rm2a, r3=r3a)
    g = Chain(plus=z_plus, minus=z_minus, partner=y_near, sum_plus=x_plus, sum_minus=x_minus, sum_partner=y_far,
              q=lambda d, e: ((yh + e) % 2) * 4 + (x + d) % 4,
              x=xg, w=wg, p=pg, rot=rot_g, sp1=sp1g, sm1=sm1g, sp2=sp2g, sm2=sm2g, s3=s3g,
              rp1=rp1g, rm1=rm1g, rp2=rp2g, rm2=rm2g, r3=r3g)
    chains = (g, a)
    lo, hi = pl.ds(0, NARROW), pl.ds(NARROW, NARROW)
    mine = pl.ds(pl.multiple_of(h * HALF, HALF), HALF)
    its = pl.ds(pl.multiple_of((1 - h) * HALF, HALF), HALF)

    local = [
        pltpu.make_async_copy(grads, xg.at[0], local_sem.at[0]),
        pltpu.make_async_copy(acts.at[mine], xa.at[0, :, lo], local_sem.at[1]),
        pltpu.make_async_copy(qs, wg.at[:, lo], local_sem.at[2]),
        pltpu.make_async_copy(qa, wa.at[lo], local_sem.at[3]),
    ]
    for copy in local:
        copy.start()

    pl.semaphore_wait(barrier, len(neighbours))

    send(a, "swap", acts.at[its], xa.at[0, :, hi], other)
    send(g, "own+", grads, xg.at[3], z_plus)
    send(g, "own-", grads, xg.at[1], z_minus)
    send(g, "ownp", grads, xg.at[4], y_near)
    send(a, "own+lo", acts.at[mine], xa.at[3, :, lo], x_plus)
    send(a, "own-lo", acts.at[mine], xa.at[1, :, lo], x_minus)
    send(a, "ownplo", acts.at[mine], xa.at[4, :, lo], y_far)
    arrived(a, "swap")
    send(a, "own+hi", xa.at[0, :, hi], xa.at[3, :, hi], x_plus)
    send(a, "own-hi", xa.at[0, :, hi], xa.at[1, :, hi], x_minus)
    send(a, "ownphi", xa.at[0, :, hi], xa.at[4, :, hi], y_far)
    send(g, "w", qs, wg.at[:, hi], other)
    send(a, "w", qa, wa.at[hi], other)

    def forward_own(c):
        if c is a:
            arrived(c, "own+lo", "own+hi")
        else:
            arrived(c, "own+")
        send(c, "fwd+", c.x.at[3, :, lo], c.x.at[2, :, lo], c.plus)
        if c is a:
            arrived(c, "own-lo", "own-hi")
        else:
            arrived(c, "own-")
        send(c, "fwd-", c.x.at[1, :, hi], c.x.at[2, :, hi], c.minus)

    def send_partner(c):
        if c is a:
            arrived(c, "ownplo", "ownphi")
        else:
            arrived(c, "ownp")
        send(c, "p+lo", c.x.at[4, :, lo], c.x.at[7, :, lo], c.plus)
        send(c, "p-hi", c.x.at[4, :, hi], c.x.at[5, :, hi], c.minus)
        send(c, "p+hi", c.x.at[4, :, hi], c.x.at[7, :, hi], c.plus)
        send(c, "p-lo", c.x.at[4, :, lo], c.x.at[5, :, lo], c.minus)

    def forward_partner(c):
        arrived(c, "p+lo")
        send(c, "pfwd+", c.x.at[7, :, lo], c.x.at[6, :, lo], c.plus)
        arrived(c, "p-hi")
        send(c, "pfwd-", c.x.at[5, :, hi], c.x.at[6, :, hi], c.minus)
        arrived(c, "p+hi", "p-lo")

    def multiply(c, i):
        if i == 1:
            arrived(c, "fwd+", "fwd-")
        if i == 3:
            arrived(c, "pfwd+", "pfwd-")
        two = pl.ds(2 * i, 2)
        rows = c.x[two].reshape(2 * HALF, WIDE)

        @pl.loop(0, WIDE // TILE)
        def _(n):
            cols = pl.ds(pl.multiple_of(n * TILE, TILE), TILE)
            c.p[two, :, cols] = jnp.dot(rows, c.w[:, cols], preferred_element_type=F32).reshape(2, HALF, TILE)

    def first_sums(c, i):
        two = pl.ds(2 * i, 2)
        first, second = pl.ds(0, PIECE), pl.ds(PIECE, PIECE)
        c.sp1[i, :, first] = encode(c.p[two, piece(c.q(2, 0))])
        c.sp1[i, :, second] = encode(c.p[two, piece(c.q(1, 1))])
        send(c, f"1+{i}", c.sp1.at[i], c.rp1.at[i], c.sum_plus)
        c.sm1[i, :, first] = encode(c.p[two, piece(c.q(2, 1))])
        c.sm1[i, :, second] = encode(c.p[two, piece(c.q(3, 0))])
        send(c, f"1-{i}", c.sm1.at[i], c.rm1.at[i], c.sum_minus)

    def second_sums(c, i):
        two = pl.ds(2 * i, 2)
        first = pl.ds(0, PIECE)
        arrived(c, f"1+{i}")
        c.sp2[i] = encode(c.p[two, piece(c.q(1, 0))] + decode(c.rp1[i, :, first]))
        send(c, f"2+{i}", c.sp2.at[i], c.rp2.at[i], c.sum_plus)
        arrived(c, f"1-{i}")
        c.sm2[i] = encode(c.p[two, piece(c.q(3, 1))] + decode(c.rm1[i, :, first]))
        send(c, f"2-{i}", c.sm2.at[i], c.rm2.at[i], c.sum_minus)

    def third_sums(c, i):
        two = pl.ds(2 * i, 2)
        second = pl.ds(PIECE, PIECE)
        arrived(c, f"2+{i}", f"2-{i}")
        c.s3[i] = encode(c.p[two, piece(c.q(0, 1))] + decode(c.rp1[i, :, second]) + decode(c.rm2[i]))
        send(c, f"3{i}", c.s3.at[i], c.r3.at[i], c.sum_partner)
        own = piece(c.q(0, 0))
        c.p[two, own] = c.p[two, own] + decode(c.rm1[i, :, second]) + decode(c.rp2[i])

    def finish(c, i):
        two = pl.ds(2 * i, 2)
        own = piece(c.q(0, 0))
        arrived(c, f"3{i}")
        c.rot[two, own] = (c.p[two, own] + decode(c.r3[i])).astype(BF16)
        ref = c.rot.at[two, own]
        send(c, f"g+{i}", ref, ref, c.sum_plus)
        send(c, f"g-{i}", ref, ref, c.sum_minus)
        send(c, f"gp{i}", ref, ref, c.sum_partner)

    def spread(c, i):
        arrived(c, f"g+{i}", f"g-{i}")
        ref = c.rot.at[2 * i, piece(c.q(3, 0))]
        send(c, f"gf+{i}", ref, ref, c.sum_plus)
        ref = c.rot.at[2 * i + 1, piece(c.q(1, 0))]
        send(c, f"gf-{i}", ref, ref, c.sum_minus)
        arrived(c, f"gp{i}")
        ref = c.rot.at[pl.ds(2 * i, 2), piece(c.q(0, 1))]
        send(c, f"h+{i}", ref, ref, c.sum_plus)
        send(c, f"h-{i}", ref, ref, c.sum_minus)

    def spread_partner(c, i):
        arrived(c, f"h+{i}", f"h-{i}")
        ref = c.rot.at[2 * i, piece(c.q(3, 1))]
        send(c, f"hf+{i}", ref, ref, c.sum_plus)
        ref = c.rot.at[2 * i + 1, piece(c.q(1, 1))]
        send(c, f"hf-{i}", ref, ref, c.sum_minus)

    def share(c, i):
        two = pl.ds(2 * i, 2)
        arrived(c, f"gf+{i}", f"gf-{i}", f"hf+{i}", f"hf-{i}")
        if c is a:
            send(c, f"c{i}", rot_a.at[two], rot_ao.at[two], other)
        else:
            send(c, f"c{i}", rot_g.at[two, :, hi], rot_go.at[two], other)
            for j in (2 * i, 2 * i + 1):
                gt[j, :, pl.ds(0, HALF)] = rot_g[j, :, lo].T

    def settle(c, i):
        arrived(c, f"c{i}")
        if c is g:
            for j in (2 * i, 2 * i + 1):
                gt[j, :, pl.ds(HALF, HALF)] = rot_go[j].T

    for c in chains:
        forward_own(c)
    for c in chains:
        send_partner(c)
    for copy in local:
        copy.wait()
    for c in chains:
        arrived(c, "w")
        multiply(c, 0)
        first_sums(c, 0)
    for c in chains:
        multiply(c, 1)
        first_sums(c, 1)
    for c in chains:
        forward_partner(c)
    stages = (second_sums, third_sums, finish, spread, spread_partner, share, settle)
    for c in chains:
        second_sums(c, 0)
    for c in chains:
        multiply(c, 2)
        first_sums(c, 2)
    for c in chains:
        third_sums(c, 0)
        second_sums(c, 1)
    for c in chains:
        multiply(c, 3)
        first_sums(c, 3)
    for tick in range(len(stages) + GROUPS):
        for i in range(GROUPS):
            at = tick + 2 - i
            if i == 0 and tick == 0:
                at = 2
            if 0 <= at < len(stages) and not (i == 0 and at < 2) and not (i == 1 and at < 1):
                for c in chains:
                    stages[at](c, i)

    def a_slot(t):
        return (t % 4 + 4 - x) % 4 + 4 * ((t // 4 + yh) % 2)

    def g_slot(t):
        return (t // 2 + 4 - z) % 4 + 4 * ((t + yl) % 2)

    @pl.loop(0, WIDE // TILE)
    def _(n):
        cols = pl.ds(pl.multiple_of(n * TILE, TILE), TILE)
        total = None
        for seq in range(SEQS):
            block = None
            for t in range(seq * 4, seq * 4 + 4):
                rows = jnp.concatenate([rot_a[a_slot(t), :, cols], rot_ao[a_slot(t), :, cols]], axis=0)
                term = jnp.dot(gt[g_slot(t)], rows, preferred_element_type=F32)
                block = term if block is None else block + term
            total = block * block if total is None else total + block * block
        out[:, cols] = total * (1.0 / TOKENS)

    for copy in started:
        copy.wait_send()


def on_device(acts, grads, qa, qs):
    vm = pltpu.VMEM
    sums = [vm((GROUPS, 2, 2 * PIECE, WIDE), BF16)] * 2 + [vm((GROUPS, 2, PIECE, WIDE), BF16)] * 3
    return pl.pallas_call(
        kernel,
        out_shape=jax.ShapeDtypeStruct((NARROW, WIDE), F32),
        in_specs=[pl.BlockSpec(memory_space=pl.ANY)] * 4,
        out_specs=pl.BlockSpec(memory_space=pltpu.VMEM),
        scratch_shapes=[
            vm((SHARDS, HALF, WIDE), BF16), vm((SHARDS, HALF, WIDE), BF16),
            vm((WIDE, WIDE), BF16), vm((WIDE, WIDE), BF16),
            vm((SHARDS, HALF, WIDE), F32), vm((SHARDS, HALF, WIDE), F32),
            vm((SHARDS, HALF, WIDE), BF16), vm((SHARDS, HALF, WIDE), BF16),
            vm((SHARDS, HALF, WIDE), BF16), vm((SHARDS, HALF, NARROW), BF16),
            vm((SHARDS, NARROW, 2 * HALF), BF16),
            *sums, *sums, *sums, *sums,
            pltpu.SemaphoreType.DMA((4,)),
            pltpu.SemaphoreType.DMA((160,)), pltpu.SemaphoreType.DMA((160,)),
        ],
        compiler_params=pltpu.CompilerParams(
            collective_id=0, has_side_effects=True, vmem_limit_bytes=56 * 2 ** 20),
        cost_estimate=pl.CostEstimate(flops=6442450944, bytes_accessed=5 * 2 ** 20, transcendentals=0),
        name="rotate_and_correlate",
    )(acts, grads, qa, qs)


def solution(mesh):
    return jax.shard_map(
        on_device,
        mesh=mesh,
        in_specs=(P("row", "col"), P("col", "row"), P("col", "row"), P("row", "col")),
        out_specs=P("col", "row"),
        check_vma=False,
    )
```

time: 402 us -> 90.1 us (0.22)
  waiting for transfers between devices: 363 us -> 0 us
  Pallas kernels: 0 us -> 86.8 us
  matrix products: 19.4 us -> 0 us
  between operations: 13.5 us -> 0.01 us
  other arithmetic: 5.15 us -> 0 us
    all_gather x4 -> x0, waiting for transfers between devices: 185 us -> none  [the longest x1 54.4 us: on_device(): lax.all_gather(grad_share.astype(jnp.bfloat16), 'row', axis=0, tiled=True)]
    reduce_scatter x2 -> x0, waiting for transfers between devices: 177 us -> none  [the longest x1 96.7 us: on_device(): lax.psum_scatter(jnp.dot(rows_part, basis_acts, preferred_element_type=jn...]
    pallas_call x0 -> x1, Pallas kernels: none -> 86.8 us  [on_device(): pl.pallas_call(kernel, out_shape=jax.ShapeDtypeStruct((NARROW, WIDE), F32...]
    dot_general x3 -> x0, matrix products: 19.4 us -> none  [the longest x1 7.16 us: on_device(): jnp.dot(rows_part, basis_acts, preferred_element_type=jnp.float32)]
  transfers between devices with their start and end apart: 6 -> 0, of which waited for: 6 -> 0; matrix products, arithmetic and copies ran while one was open for 4% -> 0% of each run, Pallas kernels for 0% -> 0%
where the time goes in v1:
time: 90.1 us; the launch traced here: 89.9 us
  Pallas kernels  86.8 us (96%)
  local copies, waits for them, and re-layouts  3.16 us (4%)
    pallas_call x1, Pallas kernels, on_device(): pl.pallas_call(kernel, out_shape=jax.ShapeDtypeStruct((NARROW, WIDE), F32...  86.8 us
    unnamed x1, local copies, waits for them, and re-layouts  3.16 us

profile of v1, /device:TPU:1, one launch (start us, length us, event | category | flops | bytes accessed | tf_op | source)
XLA Modules:
  0.0 89.9 jit_solution(4412516932280505175)
XLA Ops:
  0.0 86.8 %rotate_and_correlate.1 = f32[512,1024]{1,0:T(8,128)} custom-call(bf16[256,512]{1,0:T(8,128)(2,1)} %acts.1, bf16[128,1024]{1,0:T(8,128)(2,1)} %grads.1, bf16[512,1024]{1,0:T(8,128)(2,1)} %qa.1, bf16[1024,512]{1,0:T(8,128)(2,1)} %qs.1), custom_call_target="tpu_custom_call" | custom-call | flops 6442450944 | bytes 5242880 | tf_op jit(solution)/shard_map/rotate_and_correlate/pallas_call | solution.py:297
  86.8 3.2 %copy.6 = f32[512,1024]{1,0:T(8,128)} copy(f32[512,1024]{1,0:T(8,128)} %rotate_and_correlate.1) | data formatting | bytes 4194304

commit v2 on v0

v2 whole, which is shorter than its diff:
```python
import jax
import jax.numpy as jnp
from jax import lax
from jax.experimental import pallas as pl
from jax.experimental.pallas import tpu as pltpu
from jax.sharding import PartitionSpec as P

MESH = pl.DeviceIdType.MESH
F32, BF16 = jnp.float32, jnp.bfloat16

TOKENS, D, SEQS = 2048, 8192, 2
SHARDS = 8
HALF = TOKENS // SHARDS // 2
PIECE = HALF // SHARDS
WIDE = 1024
NARROW = WIDE // 2
TILE = 256
COPIES = 288

UP = 2.0 ** 30

GROUPS = ((0, 1), (1, 1), (2, 1), (3, 1), (4, 1), (5, 1), (6, 1), (7, 1))

ORDER = (
    "gown", "aown", "gmm0", "amm0", "gplo", "gf-", "af+", "gf+", "af-", "gmm1", "gphi", "gmm2", "g2-0", "a2-0",
    "amm2", "amm1", "aplo", "gpf+", "amm3", "g2+0", "a2+0", "gmm4", "aphi", "g2-1", "g2+1", "amm4", "g2+2", "g2-2",
    "gmm3", "gmm5", "apf+", "g30", "gpf-", "gmm6", "a2+2", "a2-2", "g2-4", "g2+4", "a2+1", "a2-1", "gfin0", "a2-3",
    "apf-", "amm5", "g31", "amm6", "g32", "a2+3", "a2-4", "a30", "gh0", "g2+3", "g2-3", "a2+4", "gmm7", "a32",
    "gfin1", "g2-5", "g2+5", "gfin2", "a31", "afin0", "g2-6", "a2+5", "ggf-0", "afin2", "a2-5", "a2+6", "g2+6",
    "gh1", "a33", "g34", "a2-6", "a34", "afin1", "ggf+0", "gh2", "amm7", "ghf-0", "ghf+0", "ah0", "agf+0", "agf-0",
    "agf-2", "g33", "ah2", "a35", "agf+2", "afin3", "a36", "g2+7", "g2-7", "ggf+1", "ggf-1", "agf-1", "agf+1",
    "gfin4", "afin4", "g35", "ah1", "a2-7", "a2+7", "ggf+2", "ggf-2", "ahf+0", "ahf-0", "gfin3", "g36", "afin5",
    "ghf+1", "ah3", "ahf+2", "ghf-1", "ahf-2", "afin6", "ghf-2", "ghf+2", "agf+3", "agf-3", "gsh0", "gh4", "ah4",
    "g37", "agf-4", "gst0", "agf+4", "ahf-1", "ahf+1", "ggf-4", "ggf+4", "gfin5", "a37", "gh3", "ash0", "ggf-3",
    "ggf+3", "gsh1", "gfin6", "ah5", "agf+5", "agf-5", "gsh2", "ast0", "ahf+3", "ahf-3", "ah6", "gst1", "ghf+4",
    "ghf-4", "ash2", "gst2", "agf-6", "agf+6", "ggf-5", "ggf+5", "gfin7", "ast2", "ghf+3", "ghf-3", "gh5", "afin7",
    "ahf-4", "ahf+4", "ash1", "ggf-6", "ggf+6", "gh6", "gsh4", "ahf+5", "ahf-5", "ast1", "gh7", "ash3", "gst4",
    "ah7", "ggf+7", "ggf-7", "gsh3", "ahf-6", "ahf+6", "ast3", "ghf-5", "ghf+5", "gst3", "agf-7", "agf+7", "ash4",
    "ghf-6", "ghf+6", "ash5", "ghf+7", "ghf-7", "ahf+7", "ahf-7", "ast4", "ash6", "ast5", "gsh5", "gsh6", "ast6",
    "gst5", "gsh7", "ash7", "gst6", "gst7", "ast7",
)


def encode(v):
    v = v * UP
    return (v * v * v).astype(BF16)


def decode(c):
    c = c.astype(F32)
    size = jnp.maximum(jnp.abs(c), 2.0 ** -126)
    return c * (jnp.exp2(jnp.log2(size) * (-2.0 / 3.0)) * (1.0 / UP))


class Chain:
    def __init__(self, **refs):
        self.__dict__.update(refs)
        self.copies = {}


def kernel(acts, grads, qa, qs, out,
           xa, xg, wa, wg, pa, pg, rot_a, rot_g, rot_ao, rot_go, gt,
           sp1a, sm1a, sp2a, sm2a, s3a, rp1a, rm1a, rp2a, rm2a, r3a,
           sp1g, sm1g, sp2g, sm2g, s3g, rp1g, rm1g, rp2g, rm2g, r3g,
           local_sem, send_sem, recv_sem):
    row, col = lax.axis_index("row"), lax.axis_index("col")
    yh, x = row // 4, row % 4
    z, yl, h = col // 4, (col // 2) % 2, col % 2

    def dev(yh, x, z, yl, h):
        return (yh * 4 + x, z * 4 + yl * 2 + h)

    x_plus, x_minus = dev(yh, (x + 1) % 4, z, yl, h), dev(yh, (x + 3) % 4, z, yl, h)
    z_plus, z_minus = dev(yh, x, (z + 1) % 4, yl, h), dev(yh, x, (z + 3) % 4, yl, h)
    y_far, y_near = dev(1 - yh, x, z, yl, h), dev(yh, x, z, 1 - yl, h)
    other = dev(yh, x, z, yl, 1 - h)
    x_plus_o, x_minus_o = dev(yh, (x + 1) % 4, z, yl, 1 - h), dev(yh, (x + 3) % 4, z, yl, 1 - h)
    y_far_o = dev(1 - yh, x, z, yl, 1 - h)

    barrier = pltpu.get_barrier_semaphore()
    neighbours = (x_plus, x_minus, z_plus, z_minus, y_far, y_near, other, x_plus_o, x_minus_o, y_far_o)
    for n in neighbours:
        pl.semaphore_signal(barrier, inc=1, device_id=n, device_id_type=MESH)

    sems = [0]

    def send(chain, name, src, dst, to):
        i = sems[0]
        sems[0] += 1
        copy = pltpu.make_async_remote_copy(
            src_ref=src, dst_ref=dst, send_sem=send_sem.at[i], recv_sem=recv_sem.at[i],
            device_id=to, device_id_type=MESH)
        copy.start()
        chain.copies[name] = copy

    def arrived(chain, *names):
        for name in names:
            copy = chain.copies.pop(name, None)
            if copy is not None:
                copy.wait()

    def piece(q):
        return pl.ds(pl.multiple_of(q * PIECE, PIECE), PIECE)

    lo, hi = pl.ds(0, NARROW), pl.ds(NARROW, NARROW)
    mine = pl.ds(pl.multiple_of(h * HALF, HALF), HALF)
    its = pl.ds(pl.multiple_of((1 - h) * HALF, HALF), HALF)
    first, second = pl.ds(0, PIECE), pl.ds(PIECE, PIECE)

    a = Chain(plus=x_plus, minus=x_minus, partner=y_far, sum_plus=z_plus, sum_minus=z_minus, sum_partner=y_near,
              plus_o=x_plus_o, minus_o=x_minus_o, partner_o=y_far_o,
              own_lo=acts.at[mine], own_hi=acts.at[its],
              q=lambda d, e: ((z + d) % 4) * 2 + (yl + e) % 2,
              x=xa, w=wa, p=pa, rot=rot_a, sp1=sp1a, sm1=sm1a, sp2=sp2a, sm2=sm2a, s3=s3a,
              rp1=rp1a, rm1=rm1a, rp2=rp2a, rm2=rm2a, r3=r3a)
    g = Chain(plus=z_plus, minus=z_minus, partner=y_near, sum_plus=x_plus, sum_minus=x_minus, sum_partner=y_far,
              plus_o=z_plus, minus_o=z_minus, partner_o=y_near,
              own_lo=grads.at[:, lo], own_hi=grads.at[:, hi],
              q=lambda d, e: ((yh + e) % 2) * 4 + (x + d) % 4,
              x=xg, w=wg, p=pg, rot=rot_g, sp1=sp1g, sm1=sm1g, sp2=sp2g, sm2=sm2g, s3=s3g,
              rp1=rp1g, rm1=rm1g, rp2=rp2g, rm2=rm2g, r3=r3g)

    local = [
        pltpu.make_async_copy(grads, xg.at[0], local_sem.at[0]),
        pltpu.make_async_copy(acts.at[mine], xa.at[0, :, lo], local_sem.at[1]),
        pltpu.make_async_copy(qs, wg.at[:, lo], local_sem.at[2]),
        pltpu.make_async_copy(qa, wa.at[lo], local_sem.at[3]),
    ]
    for copy in local:
        copy.start()

    pl.semaphore_wait(barrier, len(neighbours))

    def own(c):
        send(c, "own+lo", c.own_lo, c.x.at[2, :, lo], c.plus)
        send(c, "own-hi", c.own_hi, c.x.at[1, :, hi], c.minus_o)
        send(c, "ownplo", c.own_lo, c.x.at[4, :, lo], c.partner)
        send(c, "own+hi", c.own_hi, c.x.at[2, :, hi], c.plus_o)
        send(c, "own-lo", c.own_lo, c.x.at[1, :, lo], c.minus)
        send(c, "ownphi", c.own_hi, c.x.at[4, :, hi], c.partner_o)
        if c is a:
            send(c, "swap", acts.at[its], xa.at[0, :, hi], other)
            send(c, "w", qa, wa.at[hi], other)
        else:
            send(c, "w", qs, wg.at[:, hi], other)

    def forward_plus(c):
        arrived(c, "own+lo")
        send(c, "fwd+", c.x.at[2, :, lo], c.x.at[3, :, lo], c.plus)

    def forward_minus(c):
        arrived(c, "own-hi")
        send(c, "fwd-", c.x.at[1, :, hi], c.x.at[3, :, hi], c.minus)

    def partner_lo(c):
        arrived(c, "ownplo")
        send(c, "p+lo", c.x.at[4, :, lo], c.x.at[6, :, lo], c.plus)
        send(c, "p-lo", c.x.at[4, :, lo], c.x.at[5, :, lo], c.minus)

    def partner_hi(c):
        arrived(c, "ownphi")
        send(c, "p-hi", c.x.at[4, :, hi], c.x.at[5, :, hi], c.minus)
        send(c, "p+hi", c.x.at[4, :, hi], c.x.at[6, :, hi], c.plus)

    def partner_forward_plus(c):
        arrived(c, "p+lo")
        send(c, "pfwd+", c.x.at[6, :, lo], c.x.at[7, :, lo], c.plus)

    def partner_forward_minus(c):
        arrived(c, "p-hi")
        send(c, "pfwd-", c.x.at[5, :, hi], c.x.at[7, :, hi], c.minus)

    needs = {0: ("swap",), 1: ("own-lo", "own-hi"), 2: ("own+lo", "own+hi"), 3: ("fwd+", "fwd-"),
             4: ("ownplo", "ownphi"), 5: ("p-lo", "p-hi"), 6: ("p+lo", "p+hi"), 7: ("pfwd+", "pfwd-")}

    def slots(j):
        return pl.ds(*GROUPS[j])

    def multiply(c, j):
        start, count = GROUPS[j]
        if j == 0:
            for copy in (local[0], local[2]) if c is g else (local[1], local[3]):
                copy.wait()
        arrived(c, "w")
        for slot in range(start, start + count):
            arrived(c, *needs[slot])

        @pl.loop(0, WIDE // TILE)
        def _(n):
            cols = pl.ds(pl.multiple_of(n * TILE, TILE), TILE)
            rows = c.x[slots(j)].reshape(count * HALF, WIDE)
            sums = jnp.dot(rows, c.w[:, cols], preferred_element_type=F32)
            c.p[slots(j), :, cols] = sums.reshape(count, HALF, TILE)

        c.sp1[slots(j), first] = encode(c.p[slots(j), piece(c.q(2, 0))])
        c.sp1[slots(j), second] = encode(c.p[slots(j), piece(c.q(1, 1))])
        send(c, f"1+{j}", c.sp1.at[slots(j)], c.rp1.at[slots(j)], c.sum_plus)
        c.sm1[slots(j), first] = encode(c.p[slots(j), piece(c.q(2, 1))])
        c.sm1[slots(j), second] = encode(c.p[slots(j), piece(c.q(3, 0))])
        send(c, f"1-{j}", c.sm1.at[slots(j)], c.rm1.at[slots(j)], c.sum_minus)

    def sum_plus(c, j):
        arrived(c, f"1+{j}")
        c.sp2[slots(j)] = encode(c.p[slots(j), piece(c.q(1, 0))] + decode(c.rp1[slots(j), first]))
        send(c, f"2+{j}", c.sp2.at[slots(j)], c.rp2.at[slots(j)], c.sum_plus)

    def sum_minus(c, j):
        arrived(c, f"1-{j}")
        c.sm2[slots(j)] = encode(c.p[slots(j), piece(c.q(3, 1))] + decode(c.rm1[slots(j), first]))
        send(c, f"2-{j}", c.sm2.at[slots(j)], c.rm2.at[slots(j)], c.sum_minus)

    def sum_partner(c, j):
        arrived(c, f"2+{j}", f"2-{j}")
        c.s3[slots(j)] = encode(c.p[slots(j), piece(c.q(0, 1))] + decode(c.rp1[slots(j), second]) + decode(c.rm2[slots(j)]))
        send(c, f"3{j}", c.s3.at[slots(j)], c.r3.at[slots(j)], c.sum_partner)
        at = piece(c.q(0, 0))
        c.p[slots(j), at] = c.p[slots(j), at] + decode(c.rm1[slots(j), second]) + decode(c.rp2[slots(j)])

    def finish(c, j):
        at = piece(c.q(0, 0))
        arrived(c, f"3{j}")
        c.rot[slots(j), at] = (c.p[slots(j), at] + decode(c.r3[slots(j)])).astype(BF16)
        ref = c.rot.at[slots(j), at]
        send(c, f"g+{j}", ref, ref, c.sum_plus)
        send(c, f"g-{j}", ref, ref, c.sum_minus)
        send(c, f"gp{j}", ref, ref, c.sum_partner)

    def spread_plus(c, j):
        arrived(c, f"g+{j}")
        ref = c.rot.at[slots(j), piece(c.q(3, 0)), lo]
        send(c, f"gf+{j}", ref, ref, c.sum_plus)

    def spread_minus(c, j):
        arrived(c, f"g-{j}")
        ref = c.rot.at[slots(j), piece(c.q(1, 0)), hi]
        send(c, f"gf-{j}", ref, ref, c.sum_minus)

    def spread_partner(c, j):
        arrived(c, f"gp{j}")
        ref = c.rot.at[slots(j), piece(c.q(0, 1))]
        send(c, f"h+{j}", ref, ref, c.sum_plus)
        send(c, f"h-{j}", ref, ref, c.sum_minus)

    def spread_partner_plus(c, j):
        arrived(c, f"h+{j}")
        ref = c.rot.at[slots(j), piece(c.q(3, 1)), lo]
        send(c, f"hf+{j}", ref, ref, c.sum_plus)

    def spread_partner_minus(c, j):
        arrived(c, f"h-{j}")
        ref = c.rot.at[slots(j), piece(c.q(1, 1)), hi]
        send(c, f"hf-{j}", ref, ref, c.sum_minus)

    def share(c, j):
        arrived(c, f"gf+{j}", f"gf-{j}", f"hf+{j}", f"hf-{j}")
        if c is a:
            send(c, f"c{j}", rot_a.at[slots(j)], rot_ao.at[slots(j)], other)
        else:
            send(c, f"c{j}", rot_g.at[slots(j), :, hi], rot_go.at[slots(j)], other)
            for slot in range(GROUPS[j][0], sum(GROUPS[j])):
                gt[slot, :, pl.ds(0, HALF)] = rot_g[slot, :, lo].T

    def settle(c, j):
        arrived(c, f"c{j}")
        if c is g:
            for slot in range(GROUPS[j][0], sum(GROUPS[j])):
                gt[slot, :, pl.ds(HALF, HALF)] = rot_go[slot].T

    whole = {"own": own, "f+": forward_plus, "f-": forward_minus, "plo": partner_lo, "phi": partner_hi,
             "pf+": partner_forward_plus, "pf-": partner_forward_minus}
    slotted = {"mm": multiply, "2+": sum_plus, "2-": sum_minus, "3": sum_partner, "fin": finish,
               "gf+": spread_plus, "gf-": spread_minus, "h": spread_partner,
               "hf+": spread_partner_plus, "hf-": spread_partner_minus, "sh": share, "st": settle}
    for step in ORDER:
        c = a if step[0] == "a" else g
        if step[1:] in whole:
            whole[step[1:]](c)
        else:
            slotted[step[1:-1]](c, int(step[-1]))
    for c in (a, g):
        arrived(c, *c.copies.copy())

    def ring_slot(up):
        return up + (up // 2) * (1 - 2 * (up % 2))

    def a_slot(t):
        return ring_slot((t % 4 + 4 - x) % 4) + 4 * ((t // 4 + yh) % 2)

    def g_slot(t):
        return ring_slot((t // 2 + 4 - z) % 4) + 4 * ((t + yl) % 2)

    @pl.loop(0, WIDE // TILE)
    def _(n):
        cols = pl.ds(pl.multiple_of(n * TILE, TILE), TILE)
        total = None
        for seq in range(SEQS):
            block = None
            for t in range(seq * 4, seq * 4 + 4):
                rows = jnp.concatenate([rot_a[a_slot(t), :, cols], rot_ao[a_slot(t), :, cols]], axis=0)
                term = jnp.dot(gt[g_slot(t)], rows, preferred_element_type=F32)
                block = term if block is None else block + term
            total = block * block if total is None else total + block * block
        out[:, cols] = total * (1.0 / TOKENS)


def on_device(acts, grads, qa, qs):
    vm = pltpu.VMEM
    sums = [vm((SHARDS, 2 * PIECE, WIDE), BF16)] * 2 + [vm((SHARDS, PIECE, WIDE), BF16)] * 3
    args = [pltpu.with_memory_space_constraint(v, pltpu.HBM) for v in (acts, grads, qa, qs)]
    return pl.pallas_call(
        kernel,
        out_shape=jax.ShapeDtypeStruct((NARROW, WIDE), F32),
        in_specs=[pl.BlockSpec(memory_space=pl.ANY)] * 4,
        out_specs=pl.BlockSpec(memory_space=pltpu.VMEM),
        scratch_shapes=[
            vm((SHARDS, HALF, WIDE), BF16), vm((SHARDS, HALF, WIDE), BF16),
            vm((WIDE, WIDE), BF16), vm((WIDE, WIDE), BF16),
            vm((SHARDS, HALF, WIDE), F32), vm((SHARDS, HALF, WIDE), F32),
            vm((SHARDS, HALF, WIDE), BF16), vm((SHARDS, HALF, WIDE), BF16),
            vm((SHARDS, HALF, WIDE), BF16), vm((SHARDS, HALF, NARROW), BF16),
            vm((SHARDS, NARROW, 2 * HALF), BF16),
            *sums, *sums, *sums, *sums,
            pltpu.SemaphoreType.DMA((4,)),
            pltpu.SemaphoreType.DMA((COPIES,)), pltpu.SemaphoreType.DMA((COPIES,)),
        ],
        compiler_params=pltpu.CompilerParams(
            collective_id=0, has_side_effects=True, vmem_limit_bytes=44 * 2 ** 20),
        cost_estimate=pl.CostEstimate(flops=6442450944, bytes_accessed=5 * 2 ** 20, transcendentals=0),
        name="rotate_and_correlate",
    )(*args)


def solution(mesh):
    return jax.shard_map(
        on_device,
        mesh=mesh,
        in_specs=(P("row", "col"), P("col", "row"), P("col", "row"), P("row", "col")),
        out_specs=P("col", "row"),
        check_vma=False,
    )
```

time: 402 us -> 77.7 us (0.19)
  waiting for transfers between devices: 363 us -> 0 us
  Pallas kernels: 0 us -> 76.3 us
  matrix products: 19.4 us -> 0 us
  between operations: 13.5 us -> 0.01 us
  other arithmetic: 5.15 us -> 0 us
    all_gather x4 -> x0, waiting for transfers between devices: 185 us -> none  [the longest x1 54.4 us: on_device(): lax.all_gather(grad_share.astype(jnp.bfloat16), 'row', axis=0, tiled=True)]
    reduce_scatter x2 -> x0, waiting for transfers between devices: 177 us -> none  [the longest x1 96.7 us: on_device(): lax.psum_scatter(jnp.dot(rows_part, basis_acts, preferred_element_type=jn...]
    pallas_call x0 -> x1, Pallas kernels: none -> 76.3 us  [on_device(): pl.pallas_call(kernel, out_shape=jax.ShapeDtypeStruct((NARROW, WIDE), F32...]
    dot_general x3 -> x0, matrix products: 19.4 us -> none  [the longest x1 7.16 us: on_device(): jnp.dot(rows_part, basis_acts, preferred_element_type=jnp.float32)]
  transfers between devices with their start and end apart: 6 -> 0, of which waited for: 6 -> 0; matrix products, arithmetic and copies ran while one was open for 4% -> 0% of each run, Pallas kernels for 0% -> 0%
where the time goes in v2:
time: 77.7 us; the launch traced here: 77.6 us
  Pallas kernels  76.3 us (98%)
  local copies, waits for them, and re-layouts  1.32 us (2%)
    pallas_call x1, Pallas kernels, on_device(): pl.pallas_call(kernel, out_shape=jax.ShapeDtypeStruct((NARROW, WIDE), F32...  76.3 us

profile of v2, /device:TPU:1, one launch (start us, length us, event | category | flops | bytes accessed | tf_op | source)
XLA Modules:
  0.0 77.6 jit_solution(9705367478399557848)
XLA Ops:
  0.0 76.3 %rotate_and_correlate.1 = f32[512,1024]{1,0:T(8,128)S(1)} custom-call(bf16[256,512]{1,0:T(8,128)(2,1)} %acts.1, bf16[128,1024]{1,0:T(8,128)(2,1)} %grads.1, bf16[512,1024]{1,0:T(8,128)(2,1)} %qa.1, bf16[1024,512]{1,0:T(8,128)(2,1)} %qs.1), custom_call_target="tpu_custom_call" | custom-call | flops 6442450944 | bytes 5242880 | tf_op jit(solution)/shard_map/rotate_and_correlate/pallas_call | solution.py:310
  76.3 1.3 %copy.6 = f32[512,1024]{1,0:T(8,128)} copy(f32[512,1024]{1,0:T(8,128)S(1)} %rotate_and_correlate.1) | data formatting | bytes 4194304

commit v3 on v0

v3 whole, which is shorter than its diff:
```python
import jax
import jax.numpy as jnp
from jax import lax
from jax.experimental import pallas as pl
from jax.experimental.pallas import tpu as pltpu
from jax.sharding import PartitionSpec as P

MESH = pl.DeviceIdType.MESH
F32, BF16 = jnp.float32, jnp.bfloat16

TOKENS, D, SEQS = 2048, 8192, 2
SLOTS = 8
HALF = TOKENS // SLOTS // 2
PIECE = HALF // SLOTS
WIDE = 1024
NARROW = WIDE // 2
TILE = 512
ARRIVALS = 160
SENT = 8000

UP = 2.0 ** 30

ORDER = (
    0, 1000, 70, 1070, 30, 20, 10, 1010, 1020, 40, 71, 1071, 72, 74, 1072, 80, 1030, 1080, 50, 1073, 1040, 81, 1074,
    73, 82, 84, 90, 76, 60, 75, 1081, 1082, 1050, 1090, 100, 1076, 1060, 1075, 1100, 91, 1083, 83, 120, 92, 77, 94,
    1091, 1084, 1120, 86, 1092, 101, 1086, 85, 102, 1085, 1101, 104, 1110, 1102, 1093, 110, 1077, 121, 1130, 93, 1094,
    122, 1121, 130, 1096, 1095, 1122, 87, 1111, 124, 1103, 96, 1112, 111, 103, 1104, 95, 1087, 1106, 112, 1140, 1105,
    114, 1131, 1123, 1150, 1132, 131, 132, 1113, 106, 140, 123, 1124, 97, 1114, 150, 134, 1097, 105, 1126, 1116, 113,
    1125, 1115, 1141, 141, 1133, 142, 126, 1142, 116, 1151, 151, 107, 1107, 152, 133, 1134, 1152, 144, 125, 115, 1136,
    154, 136, 1135, 1143, 117, 127, 1127, 143, 1117, 1144, 1153, 135, 1146, 153, 1145, 146, 1154, 160, 137, 1137,
    1156, 1155, 156, 145, 155, 161, 147, 1147, 157, 1157, 162,
)


def encode(v):
    v = v * UP
    return (v * v * v).astype(BF16)


def decode(c):
    c = c.astype(F32)
    size = jnp.maximum(jnp.abs(c), 2.0 ** -126)
    return c * (jnp.exp2(jnp.log2(size) * (-2.0 / 3.0)) * (1.0 / UP))


class Chain:
    def __init__(self, **refs):
        self.__dict__.update(refs)


def kernel(acts, grads, qa, qs, out, total,
           xa, xg, wa, wg, pa, pg, rot_a, rot_g, rot_ao, rot_go,
           s1a, r1a, s2a, r2a, s3a, r3a, s1g, r1g, s2g, r2g, s3g, r3g,
           local_sem, send_sem, recv_sem):
    row, col = lax.axis_index("row"), lax.axis_index("col")
    yh, x = row // 4, row % 4
    z, yl, h = col // 4, (col // 2) % 2, col % 2

    def dev(dyh, dx, dz, dyl, core):
        return ((yh + dyh) % 2 * 4 + (x + dx) % 4, (z + dz) % 4 * 4 + (yl + dyl) % 2 * 2 + core)

    x_plus, x_minus = dev(0, 1, 0, 0, h), dev(0, 3, 0, 0, h)
    z_plus, z_minus = dev(0, 0, 1, 0, h), dev(0, 0, 3, 0, h)
    y_far, y_near = dev(1, 0, 0, 0, h), dev(0, 0, 0, 1, h)
    other = dev(0, 0, 0, 0, 1 - h)
    x_plus_o, x_minus_o, y_far_o = dev(0, 1, 0, 0, 1 - h), dev(0, 3, 0, 0, 1 - h), dev(1, 0, 0, 0, 1 - h)

    barrier = pltpu.get_barrier_semaphore()
    neighbours = (x_plus, x_minus, z_plus, z_minus, y_far, y_near, other, x_plus_o, x_minus_o, y_far_o)
    for n in neighbours:
        pl.semaphore_signal(barrier, inc=1, device_id=n, device_id_type=MESH)

    names = {}

    def arrival(c, name):
        return recv_sem.at[names.setdefault((c.at,) + name, len(names))]

    def send(c, name, src, dst, to):
        pltpu.make_async_remote_copy(
            src_ref=src, dst_ref=dst, send_sem=send_sem, recv_sem=arrival(c, name),
            device_id=to, device_id_type=MESH).start()

    def arrived(c, name, ref):
        pltpu.make_async_remote_copy(
            src_ref=ref, dst_ref=ref, send_sem=send_sem, recv_sem=arrival(c, name),
            device_id=other, device_id_type=MESH).wait_recv()

    def piece(q):
        return pl.ds(pl.multiple_of(q * PIECE, PIECE), PIECE)

    lo, hi = pl.ds(0, NARROW), pl.ds(NARROW, NARROW)
    mine = pl.ds(pl.multiple_of(h * HALF, HALF), HALF)
    its = pl.ds(pl.multiple_of((1 - h) * HALF, HALF), HALF)
    first, second = pl.ds(0, PIECE), pl.ds(PIECE, PIECE)

    a = Chain(at=1, plus=x_plus, minus=x_minus, partner=y_far, sum_plus=z_plus, sum_minus=z_minus, sum_partner=y_near,
              plus_o=x_plus_o, minus_o=x_minus_o, partner_o=y_far_o,
              own_lo=acts.at[mine], own_hi=acts.at[its],
              q=lambda d, e: ((z + d) % 4) * 2 + (yl + e) % 2,
              x=xa, w=wa, p=pa, rot=rot_a, s1=s1a, r1=r1a, s2=s2a, r2=r2a, s3=s3a, r3=r3a)
    g = Chain(at=0, plus=z_plus, minus=z_minus, partner=y_near, sum_plus=x_plus, sum_minus=x_minus, sum_partner=y_far,
              plus_o=z_plus, minus_o=z_minus, partner_o=y_near,
              own_lo=grads.at[:, lo], own_hi=grads.at[:, hi],
              q=lambda d, e: ((yh + e) % 2) * 4 + (x + d) % 4,
              x=xg, w=wg, p=pg, rot=rot_g, s1=s1g, r1=r1g, s2=s2g, r2=r2g, s3=s3g, r3=r3g)

    local = [
        pltpu.make_async_copy(grads, xg.at[0], local_sem.at[0]),
        pltpu.make_async_copy(acts.at[mine], xa.at[0, :, lo], local_sem.at[1]),
        pltpu.make_async_copy(qs, wg.at[:, lo], local_sem.at[2]),
        pltpu.make_async_copy(qa, wa.at[lo], local_sem.at[3]),
    ]
    for copy in local:
        copy.start()

    pl.semaphore_wait(barrier, len(neighbours))

    UPWARD, DOWNWARD, SIDE = 0, 1, 2
    OWN, AHEAD, PARTNER, PARTNER_AHEAD, SWAP, BASIS, FIRST, SECOND, THIRD, DONE, ACROSS, HALVES, SHARED = range(13)

    def own(c):
        send(c, (OWN, UPWARD, 0), c.own_lo, c.x.at[2, :, lo], c.plus)
        send(c, (OWN, DOWNWARD, 1), c.own_hi, c.x.at[1, :, hi], c.minus_o)
        send(c, (OWN, SIDE, 0), c.own_lo, c.x.at[4, :, lo], c.partner)
        send(c, (OWN, UPWARD, 1), c.own_hi, c.x.at[2, :, hi], c.plus_o)
        send(c, (OWN, DOWNWARD, 0), c.own_lo, c.x.at[1, :, lo], c.minus)
        send(c, (OWN, SIDE, 1), c.own_hi, c.x.at[4, :, hi], c.partner_o)
        if c is a:
            send(c, (SWAP,), acts.at[its], xa.at[0, :, hi], other)
            send(c, (BASIS,), qa, wa.at[hi], other)
            out[...] = jnp.zeros_like(out)
        else:
            send(c, (BASIS,), qs, wg.at[:, hi], other)

    def forward_up(c):
        arrived(c, (OWN, UPWARD, 0), c.x.at[2, :, lo])
        send(c, (AHEAD,), c.x.at[2, :, lo], c.x.at[3, :, lo], c.plus)

    def forward_down(c):
        arrived(c, (OWN, DOWNWARD, 1), c.x.at[1, :, hi])
        send(c, (AHEAD,), c.x.at[1, :, hi], c.x.at[3, :, hi], c.minus)

    def partner_lo(c):
        arrived(c, (OWN, SIDE, 0), c.x.at[4, :, lo])
        send(c, (PARTNER, UPWARD, 0), c.x.at[4, :, lo], c.x.at[6, :, lo], c.plus)
        send(c, (PARTNER, DOWNWARD, 0), c.x.at[4, :, lo], c.x.at[5, :, lo], c.minus)

    def partner_hi(c):
        arrived(c, (OWN, SIDE, 1), c.x.at[4, :, hi])
        send(c, (PARTNER, DOWNWARD, 1), c.x.at[4, :, hi], c.x.at[5, :, hi], c.minus)
        send(c, (PARTNER, UPWARD, 1), c.x.at[4, :, hi], c.x.at[6, :, hi], c.plus)

    def partner_forward_up(c):
        arrived(c, (PARTNER, UPWARD, 0), c.x.at[6, :, lo])
        send(c, (PARTNER_AHEAD,), c.x.at[6, :, lo], c.x.at[7, :, lo], c.plus)

    def partner_forward_down(c):
        arrived(c, (PARTNER, DOWNWARD, 1), c.x.at[5, :, hi])
        send(c, (PARTNER_AHEAD,), c.x.at[5, :, hi], c.x.at[7, :, hi], c.minus)

    needs = {1: ((OWN, DOWNWARD, 0), lo), 2: ((OWN, UPWARD, 1), hi), 3: ((AHEAD,), None),
             5: ((PARTNER, DOWNWARD, 0), lo), 6: ((PARTNER, UPWARD, 1), hi), 7: ((PARTNER_AHEAD,), None)}
    begun = set()

    def multiply(c, j):
        if c.at not in begun:
            begun.add(c.at)
            for copy in (local[0], local[2]) if c is g else (local[1], local[3]):
                copy.wait()
            arrived(c, (BASIS,), c.w.at[hi])
        if j == 0 and c is a:
            arrived(c, (SWAP,), c.x.at[0, :, hi])
        if j in needs:
            name, cols = needs[j]
            arrived(c, name, c.x.at[j] if cols is None else c.x.at[j, :, cols])

        @pl.loop(0, WIDE // TILE)
        def _(n):
            cols = pl.ds(pl.multiple_of(n * TILE, TILE), TILE)
            c.p[j, :, cols] = jnp.dot(c.x[j], c.w[:, cols], preferred_element_type=F32)

        c.s1[j, UPWARD, first] = encode(c.p[j, piece(c.q(2, 0))])
        c.s1[j, UPWARD, second] = encode(c.p[j, piece(c.q(1, 1))])
        send(c, (FIRST, j), c.s1.at[j, UPWARD], c.r1.at[j, UPWARD], c.sum_plus)
        c.s1[j, DOWNWARD, first] = encode(c.p[j, piece(c.q(2, 1))])
        c.s1[j, DOWNWARD, second] = encode(c.p[j, piece(c.q(3, 0))])
        send(c, (FIRST, j), c.s1.at[j, DOWNWARD], c.r1.at[j, DOWNWARD], c.sum_minus)

    def sum_second(c, j):
        arrived(c, (FIRST, j), c.r1.at[j])
        c.s2[j, UPWARD] = encode(c.p[j, piece(c.q(1, 0))] + decode(c.r1[j, UPWARD, first]))
        send(c, (SECOND, j), c.s2.at[j, UPWARD], c.r2.at[j, UPWARD], c.sum_plus)
        c.s2[j, DOWNWARD] = encode(c.p[j, piece(c.q(3, 1))] + decode(c.r1[j, DOWNWARD, first]))
        send(c, (SECOND, j), c.s2.at[j, DOWNWARD], c.r2.at[j, DOWNWARD], c.sum_minus)

    def sum_partner(c, j):
        arrived(c, (SECOND, j), c.r2.at[j])
        c.s3[j] = encode(c.p[j, piece(c.q(0, 1))] + decode(c.r1[j, UPWARD, second]) + decode(c.r2[j, DOWNWARD]))
        send(c, (THIRD, j), c.s3.at[j], c.r3.at[j], c.sum_partner)
        at = piece(c.q(0, 0))
        c.p[j, at] = c.p[j, at] + decode(c.r1[j, DOWNWARD, second]) + decode(c.r2[j, UPWARD])

    def finish(c, j):
        at = piece(c.q(0, 0))
        arrived(c, (THIRD, j), c.r3.at[j])
        c.rot[j, at] = (c.p[j, at] + decode(c.r3[j])).astype(BF16)
        ref = c.rot.at[j, at]
        send(c, (DONE, j), ref, ref, c.sum_plus)
        send(c, (DONE, j), ref, ref, c.sum_minus)
        send(c, (DONE, SIDE, j), ref, ref, c.sum_partner)

    def spread(c, j):
        arrived(c, (DONE, j), c.rot.at[j, pl.ds(0, 2 * PIECE)])
        ref = c.rot.at[j, piece(c.q(3, 0)), lo]
        send(c, (HALVES, j), ref, ref, c.sum_plus)
        ref = c.rot.at[j, piece(c.q(1, 0)), hi]
        send(c, (HALVES, j), ref, ref, c.sum_minus)

    def across(c, j):
        arrived(c, (DONE, SIDE, j), c.rot.at[j, first])
        ref = c.rot.at[j, piece(c.q(0, 1))]
        send(c, (ACROSS, j), ref, ref, c.sum_plus)
        send(c, (ACROSS, j), ref, ref, c.sum_minus)

    def spread_across(c, j):
        arrived(c, (ACROSS, j), c.rot.at[j, pl.ds(0, 2 * PIECE)])
        ref = c.rot.at[j, piece(c.q(3, 1)), lo]
        send(c, (HALVES, j), ref, ref, c.sum_plus)
        ref = c.rot.at[j, piece(c.q(1, 1)), hi]
        send(c, (HALVES, j), ref, ref, c.sum_minus)

    def share(c, j):
        arrived(c, (HALVES, j), c.rot.at[j, pl.ds(0, 2 * PIECE)])
        if c is a:
            send(c, (SHARED, j), rot_a.at[j], rot_ao.at[j], other)
        else:
            send(c, (SHARED, j), rot_g.at[j, :, hi], rot_go.at[j], other)

    def receive(c, j):
        arrived(c, (SHARED, j), rot_ao.at[j] if c is a else rot_go.at[j])

    def ring_slot(up):
        return up + (up // 2) * (1 - 2 * (up % 2))

    def a_slot(t):
        return ring_slot((t % 4 + 4 - x) % 4) + 4 * ((t // 4 + yh) % 2)

    def g_slot(t):
        return ring_slot((t // 2 + 4 - z) % 4) + 4 * ((t + yl) % 2)

    def correlate(above, upto):
        @pl.loop(0, SLOTS)
        def _(t):
            last = jnp.maximum(a_slot(t), g_slot(t))

            @pl.when((last > above) & (last <= upto))
            def _():
                rows = jnp.concatenate([rot_g[g_slot(t), :, lo], rot_go[g_slot(t)]], axis=0)
                columns = jnp.concatenate([rot_a[a_slot(t)], rot_ao[a_slot(t)]], axis=0)
                out[t // 4] += lax.dot_general(
                    rows, columns, (((0,), (0,)), ((), ())), preferred_element_type=F32)

    steps = (own, forward_up, forward_down, partner_lo, partner_hi, partner_forward_up, partner_forward_down,
             multiply, sum_second, sum_partner, finish, spread, across, spread_across, share, receive)
    levels = (-1, 4, 6, 7)
    for code in ORDER:
        c, step, j = (g, a)[code // 1000], code % 1000 // 10, code % 10
        if step < 7:
            steps[step](c)
        elif step < len(steps):
            steps[step](c, j)
        else:
            correlate(levels[j], levels[j + 1])
    pltpu.make_async_copy(total, total, send_sem).wait()


def on_device(acts, grads, qa, qs):
    vm = pltpu.VMEM
    sums = [vm((SLOTS, 2, 2 * PIECE, WIDE), BF16)] * 2 + [vm((SLOTS, 2, PIECE, WIDE), BF16)] * 2
    sums += [vm((SLOTS, PIECE, WIDE), BF16)] * 2
    args = [pltpu.with_memory_space_constraint(v, pltpu.HBM) for v in (acts, grads, qa, qs)]
    blocks, _ = pl.pallas_call(
        kernel,
        out_shape=(jax.ShapeDtypeStruct((SEQS, NARROW, WIDE), F32), pltpu.HBM((SENT, WIDE), BF16)),
        in_specs=[pl.BlockSpec(memory_space=pl.ANY)] * 4,
        out_specs=(pl.BlockSpec(memory_space=pltpu.VMEM), pl.BlockSpec(memory_space=pltpu.HBM)),
        scratch_shapes=[
            vm((SLOTS, HALF, WIDE), BF16), vm((SLOTS, HALF, WIDE), BF16),
            vm((WIDE, WIDE), BF16), vm((WIDE, WIDE), BF16),
            vm((SLOTS, HALF, WIDE), F32), vm((SLOTS, HALF, WIDE), F32),
            vm((SLOTS, HALF, WIDE), BF16), vm((SLOTS, HALF, WIDE), BF16),
            vm((SLOTS, HALF, WIDE), BF16), vm((SLOTS, HALF, NARROW), BF16),
            *sums, *sums,
            pltpu.SemaphoreType.DMA((4,)),
            pltpu.SemaphoreType.DMA, pltpu.SemaphoreType.DMA((ARRIVALS,)),
        ],
        compiler_params=pltpu.CompilerParams(
            collective_id=0, has_side_effects=True, vmem_limit_bytes=44 * 2 ** 20),
        cost_estimate=pl.CostEstimate(flops=6442450944, bytes_accessed=5 * 2 ** 20, transcendentals=0),
        name="rotate_and_correlate",
    )(*args)
    return (blocks[0] * blocks[0] + blocks[1] * blocks[1]) * (1.0 / TOKENS)


def solution(mesh):
    return jax.shard_map(
        on_device,
        mesh=mesh,
        in_specs=(P("row", "col"), P("col", "row"), P("col", "row"), P("row", "col")),
        out_specs=P("col", "row"),
        check_vma=False,
    )
```

time: 402 us -> 72.6 us (0.18)
  waiting for transfers between devices: 363 us -> 0 us
  Pallas kernels: 0 us -> 70.5 us
  matrix products: 19.4 us -> 0 us
  between operations: 13.5 us -> 0.01 us
    all_gather x4 -> x0, waiting for transfers between devices: 185 us -> none  [the longest x1 54.4 us: on_device(): lax.all_gather(grad_share.astype(jnp.bfloat16), 'row', axis=0, tiled=True)]
    reduce_scatter x2 -> x0, waiting for transfers between devices: 177 us -> none  [the longest x1 96.7 us: on_device(): lax.psum_scatter(jnp.dot(rows_part, basis_acts, preferred_element_type=jn...]
    pallas_call x0 -> x1, Pallas kernels: none -> 70.5 us  [on_device(): pl.pallas_call(kernel, out_shape=(jax.ShapeDtypeStruct((SEQS, NARROW, WID...]
    dot_general x3 -> x0, matrix products: 19.4 us -> none  [the longest x1 7.16 us: on_device(): jnp.dot(rows_part, basis_acts, preferred_element_type=jnp.float32)]
  transfers between devices with their start and end apart: 6 -> 0, of which waited for: 6 -> 0; matrix products, arithmetic and copies ran while one was open for 4% -> 0% of each run, Pallas kernels for 0% -> 0%
where the time goes in v3:
time: 72.6 us; the launch traced here: 72.5 us
  Pallas kernels  70.5 us (97%)
  other arithmetic  1.99 us (3%)
    pallas_call x1, Pallas kernels, on_device(): pl.pallas_call(kernel, out_shape=(jax.ShapeDtypeStruct((SEQS, NARROW, WID...  70.5 us
    mul x1, other arithmetic, on_device(): return (blocks[0] * blocks[0] + blocks[1] * blocks[1]) * (1.0 / TOKENS)  1.99 us

profile of v3, /device:TPU:1, one launch (start us, length us, event | category | flops | bytes accessed | tf_op | source)
XLA Modules:
  0.0 72.5 jit_solution(1541852566360357080)
XLA Ops:
  0.0 70.5 %rotate_and_correlate.1 = (f32[2,512,1024]{2,1,0:T(8,128)S(1)}, bf16[8000,1024]{1,0:T(8,128)(2,1)}) custom-call(bf16[256,512]{1,0:T(8,128)(2,1)} %acts.1, bf16[128,1024]{1,0:T(8,128)(2,1)} %grads.1, bf16[512,1024]{1,0:T(8,128)(2,1)} %qa.1, bf16[1024,512]{1,0:T(8,128)(2,1)} %qs.1), custom_call_target="tpu_custom_call" | custom-call | flops 6442450944 | bytes 5242880 | tf_op jit(solution)/shard_map/rotate_and_correlate/pallas_call | solution.py:282
  70.5 2.0 %multiply_bitcast_fusion = f32[512,1024]{1,0:T(8,128)} fusion(f32[2,512,1024]{2,1,0:T(8,128)S(1)} %get-tuple-element.6), kind=kLoop, calls=%fused_computation | loop fusion | flops 2097152 | bytes 6291456 | tf_op jit(solution)/shard_map/mul | solution.py:302

commit v4 on v3

--- a/solution.py
+++ b/solution.py
@@ -15,20 +15,22 @@
 WIDE = 1024
 NARROW = WIDE // 2
 TILE = 512
+DIRECT = (6, 7)
+ASIDE = (3,)
 ARRIVALS = 160
 SENT = 8000
 
 UP = 2.0 ** 30
 
 ORDER = (
-    0, 1000, 70, 1070, 30, 20, 10, 1010, 1020, 40, 71, 1071, 72, 74, 1072, 80, 1030, 1080, 50, 1073, 1040, 81, 1074,
-    73, 82, 84, 90, 76, 60, 75, 1081, 1082, 1050, 1090, 100, 1076, 1060, 1075, 1100, 91, 1083, 83, 120, 92, 77, 94,
-    1091, 1084, 1120, 86, 1092, 101, 1086, 85, 102, 1085, 1101, 104, 1110, 1102, 1093, 110, 1077, 121, 1130, 93, 1094,
-    122, 1121, 130, 1096, 1095, 1122, 87, 1111, 124, 1103, 96, 1112, 111, 103, 1104, 95, 1087, 1106, 112, 1140, 1105,
-    114, 1131, 1123, 1150, 1132, 131, 132, 1113, 106, 140, 123, 1124, 97, 1114, 150, 134, 1097, 105, 1126, 1116, 113,
-    1125, 1115, 1141, 141, 1133, 142, 126, 1142, 116, 1151, 151, 107, 1107, 152, 133, 1134, 1152, 144, 125, 115, 1136,
-    154, 136, 1135, 1143, 117, 127, 1127, 143, 1117, 1144, 1153, 135, 1146, 153, 1145, 146, 1154, 160, 137, 1137,
-    1156, 1155, 156, 145, 155, 161, 147, 1147, 157, 1157, 162,
+    0, 1000, 70, 1070, 30, 20, 10, 1010, 1020, 40, 72, 1071, 71, 1072, 1080, 80, 74, 1030, 50, 1073, 1040, 82, 1074,
+    73, 81, 90, 60, 75, 76, 1081, 1083, 84, 1050, 1082, 1090, 83, 100, 1060, 1075, 92, 1076, 1100, 91, 77, 85, 1091,
+    1084, 120, 1093, 1092, 86, 102, 1120, 94, 1085, 1101, 101, 1086, 1102, 1110, 93, 1094, 122, 110, 1103, 1077, 1121,
+    1130, 104, 87, 1095, 1122, 121, 95, 1111, 1104, 130, 1096, 96, 1112, 112, 1113, 1105, 124, 111, 103, 1087, 105,
+    1124, 132, 1131, 1106, 1140, 114, 1132, 97, 106, 1150, 131, 1114, 140, 1123, 1125, 134, 150, 170, 1115, 1097, 113,
+    1134, 1126, 125, 115, 1141, 142, 107, 1151, 152, 1142, 1143, 126, 1166, 141, 1107, 166, 144, 1135, 123, 1152,
+    1144, 1153, 135, 151, 171, 172, 154, 1154, 1146, 127, 1127, 1156, 167, 1145, 143, 1167, 146, 145, 1155, 153, 174,
+    173, 147, 155, 1147, 175, 156, 176, 1157, 157, 177,
 )
 
 
@@ -50,7 +52,7 @@
 
 def kernel(acts, grads, qa, qs, out, total,
            xa, xg, wa, wg, pa, pg, rot_a, rot_g, rot_ao, rot_go,
-           s1a, r1a, s2a, r2a, s3a, r3a, s1g, r1g, s2g, r2g, s3g, r3g,
+           s1a, r1a, s2a, r2a, s3a, r3a, s4a, r4a, s1g, r1g, s2g, r2g, s3g, r3g, s4g, r4g,
            local_sem, send_sem, recv_sem):
     row, col = lax.axis_index("row"), lax.axis_index("col")
     yh, x = row // 4, row % 4
@@ -66,7 +68,8 @@
     x_plus_o, x_minus_o, y_far_o = dev(0, 1, 0, 0, 1 - h), dev(0, 3, 0, 0, 1 - h), dev(1, 0, 0, 0, 1 - h)
 
     barrier = pltpu.get_barrier_semaphore()
-    neighbours = (x_plus, x_minus, z_plus, z_minus, y_far, y_near, other, x_plus_o, x_minus_o, y_far_o)
+    x_two, z_two = dev(0, 2, 0, 0, h), dev(0, 0, 2, 0, h)
+    neighbours = (x_plus, x_minus, z_plus, z_minus, y_far, y_near, other, x_plus_o, x_minus_o, y_far_o, x_two, z_two)
     for n in neighbours:
         pl.semaphore_signal(barrier, inc=1, device_id=n, device_id_type=MESH)
 
@@ -93,16 +96,20 @@
     its = pl.ds(pl.multiple_of((1 - h) * HALF, HALF), HALF)
     first, second = pl.ds(0, PIECE), pl.ds(PIECE, PIECE)
 
-    a = Chain(at=1, plus=x_plus, minus=x_minus, partner=y_far, sum_plus=z_plus, sum_minus=z_minus, sum_partner=y_near,
+    a = Chain(at=1, plus=x_plus, minus=x_minus, partner=y_far,
+              sum_plus=z_plus, sum_minus=z_minus, sum_two=z_two, sum_partner=y_near,
               plus_o=x_plus_o, minus_o=x_minus_o, partner_o=y_far_o,
               own_lo=acts.at[mine], own_hi=acts.at[its],
               q=lambda d, e: ((z + d) % 4) * 2 + (yl + e) % 2,
-              x=xa, w=wa, p=pa, rot=rot_a, s1=s1a, r1=r1a, s2=s2a, r2=r2a, s3=s3a, r3=r3a)
-    g = Chain(at=0, plus=z_plus, minus=z_minus, partner=y_near, sum_plus=x_plus, sum_minus=x_minus, sum_partner=y_far,
+              x=xa, w=wa, p=pa, rot=rot_a, s1=s1a, r1=r1a, s2=s2a, r2=r2a, s3=s3a, r3=r3a,
+              s4=s4a, r4=r4a)
+    g = Chain(at=0, plus=z_plus, minus=z_minus, partner=y_near,
+              sum_plus=x_plus, sum_minus=x_minus, sum_two=x_two, sum_partner=y_far,
               plus_o=z_plus, minus_o=z_minus, partner_o=y_near,
               own_lo=grads.at[:, lo], own_hi=grads.at[:, hi],
               q=lambda d, e: ((yh + e) % 2) * 4 + (x + d) % 4,
-              x=xg, w=wg, p=pg, rot=rot_g, s1=s1g, r1=r1g, s2=s2g, r2=r2g, s3=s3g, r3=r3g)
+              x=xg, w=wg, p=pg, rot=rot_g, s1=s1g, r1=r1g, s2=s2g, r2=r2g, s3=s3g, r3=r3g,
+              s4=s4g, r4=r4g)
 
     local = [
         pltpu.make_async_copy(grads, xg.at[0], local_sem.at[0]),
@@ -179,6 +186,11 @@
             cols = pl.ds(pl.multiple_of(n * TILE, TILE), TILE)
             c.p[j, :, cols] = jnp.dot(c.x[j], c.w[:, cols], preferred_element_type=F32)
 
+        if j in ASIDE:
+            for d in range(4):
+                c.s1[j, d // 2, (first, second)[d % 2]] = encode(c.p[j, piece(c.q(d, 1))])
+            send(c, (FIRST, j), c.s1.at[j], c.r1.at[j], c.sum_partner)
+            return
         c.s1[j, UPWARD, first] = encode(c.p[j, piece(c.q(2, 0))])
         c.s1[j, UPWARD, second] = encode(c.p[j, piece(c.q(1, 1))])
         send(c, (FIRST, j), c.s1.at[j, UPWARD], c.r1.at[j, UPWARD], c.sum_plus)
@@ -188,12 +200,33 @@
 
     def sum_second(c, j):
         arrived(c, (FIRST, j), c.r1.at[j])
+        if j in ASIDE:
+            for d in range(4):
+                at = piece(c.q(d, 0))
+                c.p[j, at] = c.p[j, at] + decode(c.r1[j, d // 2, (first, second)[d % 2]])
+            at = piece(c.q(2, 0))
+            c.s2[j, UPWARD, :, lo] = encode(c.p[j, at, lo])
+            c.s2[j, DOWNWARD, :, hi] = encode(c.p[j, at, hi])
+            send(c, (SECOND, j), c.s2.at[j, UPWARD, :, lo], c.r2.at[j, UPWARD, :, lo], c.sum_plus)
+            send(c, (SECOND, j), c.s2.at[j, DOWNWARD, :, hi], c.r2.at[j, DOWNWARD, :, hi], c.sum_minus)
+            return
         c.s2[j, UPWARD] = encode(c.p[j, piece(c.q(1, 0))] + decode(c.r1[j, UPWARD, first]))
         send(c, (SECOND, j), c.s2.at[j, UPWARD], c.r2.at[j, UPWARD], c.sum_plus)
         c.s2[j, DOWNWARD] = encode(c.p[j, piece(c.q(3, 1))] + decode(c.r1[j, DOWNWARD, first]))
         send(c, (SECOND, j), c.s2.at[j, DOWNWARD], c.r2.at[j, DOWNWARD], c.sum_minus)
 
     def sum_partner(c, j):
+        if j in ASIDE:
+            arrived(c, (SECOND, j), c.r2.at[j, UPWARD])
+            k = ASIDE.index(j)
+            up, down = piece(c.q(1, 0)), piece(c.q(3, 0))
+            c.s4[k, UPWARD, :, lo] = encode(c.p[j, up, lo] + decode(c.r2[j, UPWARD, :, lo]))
+            c.s4[k, UPWARD, :, hi] = encode(c.p[j, up, hi])
+            send(c, (THIRD, j), c.s4.at[k, UPWARD], c.r4.at[k, UPWARD], c.sum_plus)
+            c.s4[k, DOWNWARD, :, lo] = encode(c.p[j, down, lo])
+            c.s4[k, DOWNWARD, :, hi] = encode(c.p[j, down, hi] + decode(c.r2[j, DOWNWARD, :, hi]))
+            send(c, (THIRD, j), c.s4.at[k, DOWNWARD], c.r4.at[k, DOWNWARD], c.sum_minus)
+            return
         arrived(c, (SECOND, j), c.r2.at[j])
         c.s3[j] = encode(c.p[j, piece(c.q(0, 1))] + decode(c.r1[j, UPWARD, second]) + decode(c.r2[j, DOWNWARD]))
         send(c, (THIRD, j), c.s3.at[j], c.r3.at[j], c.sum_partner)
@@ -202,12 +235,22 @@
 
     def finish(c, j):
         at = piece(c.q(0, 0))
-        arrived(c, (THIRD, j), c.r3.at[j])
-        c.rot[j, at] = (c.p[j, at] + decode(c.r3[j])).astype(BF16)
+        if j in ASIDE:
+            k = ASIDE.index(j)
+            arrived(c, (THIRD, j), c.r4.at[k])
+            c.rot[j, at] = (c.p[j, at] + decode(c.r4[k, UPWARD]) + decode(c.r4[k, DOWNWARD])).astype(BF16)
+        else:
+            arrived(c, (THIRD, j), c.r3.at[j])
+            c.rot[j, at] = (c.p[j, at] + decode(c.r3[j])).astype(BF16)
         ref = c.rot.at[j, at]
-        send(c, (DONE, j), ref, ref, c.sum_plus)
-        send(c, (DONE, j), ref, ref, c.sum_minus)
-        send(c, (DONE, SIDE, j), ref, ref, c.sum_partner)
+        if j in DIRECT:
+            send(c, (DONE, SIDE, j), ref, ref, c.sum_partner)
+            for to in (c.sum_plus, c.sum_minus, c.sum_two):
+                send(c, (DONE, j), ref, ref, to)
+        else:
+            send(c, (DONE, j), ref, ref, c.sum_plus)
+            send(c, (DONE, j), ref, ref, c.sum_minus)
+            send(c, (DONE, SIDE, j), ref, ref, c.sum_partner)
 
     def spread(c, j):
         arrived(c, (DONE, j), c.rot.at[j, pl.ds(0, 2 * PIECE)])
@@ -215,12 +258,25 @@
         send(c, (HALVES, j), ref, ref, c.sum_plus)
         ref = c.rot.at[j, piece(c.q(1, 0)), hi]
         send(c, (HALVES, j), ref, ref, c.sum_minus)
+        if j in ASIDE:
+            for d in (3, 1):
+                ref = c.rot.at[j, piece(c.q(d, 0))]
+                send(c, (DONE, SIDE, j), ref, ref, c.sum_partner)
 
     def across(c, j):
+        if j in ASIDE:
+            arrived(c, (HALVES, j), c.rot.at[j, first])
+            ref = c.rot.at[j, piece(c.q(2, 0))]
+            send(c, (DONE, SIDE, j), ref, ref, c.sum_partner)
+            return
         arrived(c, (DONE, SIDE, j), c.rot.at[j, first])
         ref = c.rot.at[j, piece(c.q(0, 1))]
-        send(c, (ACROSS, j), ref, ref, c.sum_plus)
-        send(c, (ACROSS, j), ref, ref, c.sum_minus)
+        if j in DIRECT:
+            for to in (c.sum_two, c.sum_plus, c.sum_minus):
+                send(c, (HALVES, j), ref, ref, to)
+        else:
+            send(c, (ACROSS, j), ref, ref, c.sum_plus)
+            send(c, (ACROSS, j), ref, ref, c.sum_minus)
 
     def spread_across(c, j):
         arrived(c, (ACROSS, j), c.rot.at[j, pl.ds(0, 2 * PIECE)])
@@ -229,12 +285,28 @@
         ref = c.rot.at[j, piece(c.q(1, 1)), hi]
         send(c, (HALVES, j), ref, ref, c.sum_minus)
 
+    def share_rows(c, j, rows):
+        if c is a:
+            send(c, (SHARED, j), rot_a.at[j, rows], rot_ao.at[j, rows], other)
+        else:
+            send(c, (SHARED, j), rot_g.at[j, rows, hi], rot_go.at[j, rows], other)
+
+    def share_early(c, j):
+        arrived(c, (DONE, j), c.rot.at[j, pl.ds(0, 3 * PIECE)])
+        for d in range(4):
+            share_rows(c, j, piece(c.q(d, 0)))
+
     def share(c, j):
-        arrived(c, (HALVES, j), c.rot.at[j, pl.ds(0, 2 * PIECE)])
-        if c is a:
-            send(c, (SHARED, j), rot_a.at[j], rot_ao.at[j], other)
-        else:
-            send(c, (SHARED, j), rot_g.at[j, :, hi], rot_go.at[j], other)
+        if j in DIRECT:
+            arrived(c, (HALVES, j), c.rot.at[j, pl.ds(0, 3 * PIECE)])
+            for d in range(4):
+                share_rows(c, j, piece(c.q(d, 1)))
+            return
+        if j in ASIDE:
+            arrived(c, (DONE, SIDE, j), c.rot.at[j, pl.ds(0, 4 * PIECE)])
+        else:
+            arrived(c, (HALVES, j), c.rot.at[j, pl.ds(0, 2 * PIECE)])
+        share_rows(c, j, pl.ds(0, HALF))
 
     def receive(c, j):
         arrived(c, (SHARED, j), rot_ao.at[j] if c is a else rot_go.at[j])
@@ -261,8 +333,8 @@
                     rows, columns, (((0,), (0,)), ((), ())), preferred_element_type=F32)
 
     steps = (own, forward_up, forward_down, partner_lo, partner_hi, partner_forward_up, partner_forward_down,
-             multiply, sum_second, sum_partner, finish, spread, across, spread_across, share, receive)
-    levels = (-1, 4, 6, 7)
+             multiply, sum_second, sum_partner, finish, spread, across, spread_across, share, receive, share_early)
+    levels = (-1, 0, 1, 2, 3, 4, 5, 6, 7)
     for code in ORDER:
         c, step, j = (g, a)[code // 1000], code % 1000 // 10, code % 10
         if step < 7:
@@ -277,7 +349,7 @@
 def on_device(acts, grads, qa, qs):
     vm = pltpu.VMEM
     sums = [vm((SLOTS, 2, 2 * PIECE, WIDE), BF16)] * 2 + [vm((SLOTS, 2, PIECE, WIDE), BF16)] * 2
-    sums += [vm((SLOTS, PIECE, WIDE), BF16)] * 2
+    sums += [vm((SLOTS, PIECE, WIDE), BF16)] * 2 + [vm((max(len(ASIDE), 1), 2, PIECE, WIDE), BF16)] * 2
     args = [pltpu.with_memory_space_constraint(v, pltpu.HBM) for v in (acts, grads, qa, qs)]
     blocks, _ = pl.pallas_call(
         kernel,

time: 72.6 us -> 69.6 us (0.959)
  Pallas kernels: 70.5 us -> 67.5 us
    pallas_call x1, Pallas kernels: 70.5 us -> 67.5 us  [on_device(): pl.pallas_call(kernel, out_shape=(jax.ShapeDtypeStruct((SEQS, NARROW, WID...]
where the time goes in v4:
time: 69.6 us; the launch traced here: 69.5 us
  Pallas kernels  67.5 us (97%)
  other arithmetic  1.99 us (3%)
    pallas_call x1, Pallas kernels, on_device(): pl.pallas_call(kernel, out_shape=(jax.ShapeDtypeStruct((SEQS, NARROW, WID...  67.5 us
    mul x1, other arithmetic, on_device(): return (blocks[0] * blocks[0] + blocks[1] * blocks[1]) * (1.0 / TOKENS)  1.99 us

profile of v4, /device:TPU:1, one launch (start us, length us, event | category | flops | bytes accessed | tf_op | source)
XLA Modules:
  0.0 69.5 jit_solution(9669734942101354034)
XLA Ops:
  0.0 67.5 %rotate_and_correlate.1 = (f32[2,512,1024]{2,1,0:T(8,128)S(1)}, bf16[8000,1024]{1,0:T(8,128)(2,1)}) custom-call(bf16[256,512]{1,0:T(8,128)(2,1)} %acts.1, bf16[128,1024]{1,0:T(8,128)(2,1)} %grads.1, bf16[512,1024]{1,0:T(8,128)(2,1)} %qa.1, bf16[1024,512]{1,0:T(8,128)(2,1)} %qs.1), custom_call_target="tpu_custom_call" | custom-call | flops 6442450944 | bytes 5242880 | tf_op jit(solution)/shard_map/rotate_and_correlate/pallas_call | solution.py:354
  67.5 2.0 %multiply_bitcast_fusion = f32[512,1024]{1,0:T(8,128)} fusion(f32[2,512,1024]{2,1,0:T(8,128)S(1)} %get-tuple-element.6), kind=kLoop, calls=%fused_computation | loop fusion | flops 2097152 | bytes 6291456 | tf_op jit(solution)/shard_map/mul | solution.py:374

commit v5 on v4

--- a/solution.py
+++ b/solution.py
@@ -17,20 +17,22 @@
 TILE = 512
 DIRECT = (6, 7)
 ASIDE = (3,)
-ARRIVALS = 160
+ARRIVALS = 149
 SENT = 8000
 
+PASSES = ((-1, 0), (0, 2), (2, 4), (4, 6), (6, 7))
+
 UP = 2.0 ** 30
 
 ORDER = (
-    0, 1000, 70, 1070, 30, 20, 10, 1010, 1020, 40, 72, 1071, 71, 1072, 1080, 80, 74, 1030, 50, 1073, 1040, 82, 1074,
-    73, 81, 90, 60, 75, 76, 1081, 1083, 84, 1050, 1082, 1090, 83, 100, 1060, 1075, 92, 1076, 1100, 91, 77, 85, 1091,
-    1084, 120, 1093, 1092, 86, 102, 1120, 94, 1085, 1101, 101, 1086, 1102, 1110, 93, 1094, 122, 110, 1103, 1077, 1121,
-    1130, 104, 87, 1095, 1122, 121, 95, 1111, 1104, 130, 1096, 96, 1112, 112, 1113, 1105, 124, 111, 103, 1087, 105,
-    1124, 132, 1131, 1106, 1140, 114, 1132, 97, 106, 1150, 131, 1114, 140, 1123, 1125, 134, 150, 170, 1115, 1097, 113,
-    1134, 1126, 125, 115, 1141, 142, 107, 1151, 152, 1142, 1143, 126, 1166, 141, 1107, 166, 144, 1135, 123, 1152,
-    1144, 1153, 135, 151, 171, 172, 154, 1154, 1146, 127, 1127, 1156, 167, 1145, 143, 1167, 146, 145, 1155, 153, 174,
-    173, 147, 155, 1147, 175, 156, 176, 1157, 157, 177,
+    0, 1000, 70, 1070, 1010, 10, 1020, 20, 71, 30, 1080, 80, 72, 40, 74, 1073, 1071, 81, 1072, 1030, 1090, 73, 1040,
+    82, 1074, 1083, 1081, 50, 60, 84, 75, 91, 76, 1082, 90, 1100, 83, 1091, 92, 1084, 1050, 1060, 1075, 94, 100, 1076,
+    85, 1092, 1093, 101, 1120, 86, 1094, 1101, 77, 104, 1085, 1102, 102, 121, 1086, 1103, 1077, 95, 1104, 96, 93,
+    1095, 87, 1121, 1122, 120, 1110, 1096, 122, 1113, 105, 1087, 111, 1112, 103, 1114, 124, 1111, 1124, 1105, 110,
+    1130, 97, 1106, 131, 106, 130, 1131, 1097, 132, 113, 112, 114, 1125, 134, 1123, 1132, 125, 1134, 141, 1140, 1126,
+    107, 1107, 126, 123, 1166, 1135, 1142, 142, 1144, 140, 144, 1115, 1141, 115, 135, 1127, 127, 1143, 150, 1150, 170,
+    1152, 143, 152, 151, 167, 166, 1145, 154, 1151, 1146, 171, 146, 145, 1167, 1154, 153, 1153, 172, 1147, 156, 1156,
+    1155, 147, 155, 173, 157, 1157, 174,
 )
 
 
@@ -51,7 +53,7 @@
 
 
 def kernel(acts, grads, qa, qs, out, total,
-           xa, xg, wa, wg, pa, pg, rot_a, rot_g, rot_ao, rot_go,
+           sums, xa, xg, wa, wg, pa, pg, rot_a, rot_g, rot_ao, rot_go,
            s1a, r1a, s2a, r2a, s3a, r3a, s4a, r4a, s1g, r1g, s2g, r2g, s3g, r3g, s4g, r4g,
            local_sem, send_sem, recv_sem):
     row, col = lax.axis_index("row"), lax.axis_index("col")
@@ -135,7 +137,7 @@
         if c is a:
             send(c, (SWAP,), acts.at[its], xa.at[0, :, hi], other)
             send(c, (BASIS,), qa, wa.at[hi], other)
-            out[...] = jnp.zeros_like(out)
+            sums[...] = jnp.zeros_like(sums)
         else:
             send(c, (BASIS,), qs, wg.at[:, hi], other)
 
@@ -329,12 +331,11 @@
             def _():
                 rows = jnp.concatenate([rot_g[g_slot(t), :, lo], rot_go[g_slot(t)]], axis=0)
                 columns = jnp.concatenate([rot_a[a_slot(t)], rot_ao[a_slot(t)]], axis=0)
-                out[t // 4] += lax.dot_general(
+                sums[t // 4] += lax.dot_general(
                     rows, columns, (((0,), (0,)), ((), ())), preferred_element_type=F32)
 
     steps = (own, forward_up, forward_down, partner_lo, partner_hi, partner_forward_up, partner_forward_down,
              multiply, sum_second, sum_partner, finish, spread, across, spread_across, share, receive, share_early)
-    levels = (-1, 0, 1, 2, 3, 4, 5, 6, 7)
     for code in ORDER:
         c, step, j = (g, a)[code // 1000], code % 1000 // 10, code % 10
         if step < 7:
@@ -342,7 +343,14 @@
         elif step < len(steps):
             steps[step](c, j)
         else:
-            correlate(levels[j], levels[j + 1])
+            correlate(*PASSES[j])
+
+    @pl.loop(0, NARROW // 64)
+    def _(n):
+        rows = pl.ds(pl.multiple_of(n * 64, 64), 64)
+        out[rows] = (sums[0, rows] * sums[0, rows] + sums[1, rows] * sums[1, rows]) * (1.0 / TOKENS)
+
+    assert len(names) == ARRIVALS
     pltpu.make_async_copy(total, total, send_sem).wait()
 
 
@@ -351,12 +359,13 @@
     sums = [vm((SLOTS, 2, 2 * PIECE, WIDE), BF16)] * 2 + [vm((SLOTS, 2, PIECE, WIDE), BF16)] * 2
     sums += [vm((SLOTS, PIECE, WIDE), BF16)] * 2 + [vm((max(len(ASIDE), 1), 2, PIECE, WIDE), BF16)] * 2
     args = [pltpu.with_memory_space_constraint(v, pltpu.HBM) for v in (acts, grads, qa, qs)]
-    blocks, _ = pl.pallas_call(
+    correction, _ = pl.pallas_call(
         kernel,
-        out_shape=(jax.ShapeDtypeStruct((SEQS, NARROW, WIDE), F32), pltpu.HBM((SENT, WIDE), BF16)),
+        out_shape=(jax.ShapeDtypeStruct((NARROW, WIDE), F32), pltpu.HBM((SENT, WIDE), BF16)),
         in_specs=[pl.BlockSpec(memory_space=pl.ANY)] * 4,
         out_specs=(pl.BlockSpec(memory_space=pltpu.VMEM), pl.BlockSpec(memory_space=pltpu.HBM)),
         scratch_shapes=[
+            vm((SEQS, NARROW, WIDE), F32),
             vm((SLOTS, HALF, WIDE), BF16), vm((SLOTS, HALF, WIDE), BF16),
             vm((WIDE, WIDE), BF16), vm((WIDE, WIDE), BF16),
             vm((SLOTS, HALF, WIDE), F32), vm((SLOTS, HALF, WIDE), F32),
@@ -367,11 +376,11 @@
             pltpu.SemaphoreType.DMA, pltpu.SemaphoreType.DMA((ARRIVALS,)),
         ],
         compiler_params=pltpu.CompilerParams(
-            collective_id=0, has_side_effects=True, vmem_limit_bytes=44 * 2 ** 20),
+            collective_id=0, has_side_effects=True, vmem_limit_bytes=48 * 2 ** 20),
         cost_estimate=pl.CostEstimate(flops=6442450944, bytes_accessed=5 * 2 ** 20, transcendentals=0),
         name="rotate_and_correlate",
     )(*args)
-    return (blocks[0] * blocks[0] + blocks[1] * blocks[1]) * (1.0 / TOKENS)
+    return correction
 
 
 def solution(mesh):

time: 69.6 us -> 67.4 us (0.968)
  other arithmetic: 1.99 us -> 0 us
  Pallas kernels: 67.5 us -> 66 us
  local copies, waits for them, and re-layouts: 0 us -> 1.32 us
    mul x1 -> x0, other arithmetic: 1.99 us -> none  [on_device(): return (blocks[0] * blocks[0] + blocks[1] * blocks[1]) * (1.0 / TOKENS)]
    pallas_call x1, Pallas kernels: 67.5 us -> 66 us  [on_device(): pl.pallas_call(kernel, out_shape=(jax.ShapeDtypeStruct((NARROW, WIDE), F3...]
    unnamed x0 -> x1, local copies, waits for them, and re-layouts: none -> 1.32 us
where the time goes in v5:
time: 67.4 us; the launch traced here: 67.3 us
  Pallas kernels  66 us (98%)
  local copies, waits for them, and re-layouts  1.32 us (2%)
    pallas_call x1, Pallas kernels, on_device(): pl.pallas_call(kernel, out_shape=(jax.ShapeDtypeStruct((NARROW, WIDE), F3...  66 us

profile of v5, /device:TPU:1, one launch (start us, length us, event | category | flops | bytes accessed | tf_op | source)
XLA Modules:
  0.0 67.3 jit_solution(5763325879755752286)
XLA Ops:
  0.0 66.0 %rotate_and_correlate.1 = (f32[512,1024]{1,0:T(8,128)S(1)}, bf16[8000,1024]{1,0:T(8,128)(2,1)}) custom-call(bf16[256,512]{1,0:T(8,128)(2,1)} %acts.1, bf16[128,1024]{1,0:T(8,128)(2,1)} %grads.1, bf16[512,1024]{1,0:T(8,128)(2,1)} %qa.1, bf16[1024,512]{1,0:T(8,128)(2,1)} %qs.1), custom_call_target="tpu_custom_call" | custom-call | flops 6442450944 | bytes 5242880 | tf_op jit(solution)/shard_map/rotate_and_correlate/pallas_call | solution.py:362
  66.0 1.3 %copy.6 = f32[512,1024]{1,0:T(8,128)} copy(f32[512,1024]{1,0:T(8,128)S(1)} %get-tuple-element.6) | data formatting | bytes 4194304

commit v6 on v5

--- a/solution.py
+++ b/solution.py
@@ -16,7 +16,8 @@
 NARROW = WIDE // 2
 TILE = 512
 DIRECT = (6, 7)
-ASIDE = (3,)
+ASIDE = (2, 3)
+LATER = (3,)
 ARRIVALS = 149
 SENT = 8000
 
@@ -25,14 +26,14 @@
 UP = 2.0 ** 30
 
 ORDER = (
-    0, 1000, 70, 1070, 1010, 10, 1020, 20, 71, 30, 1080, 80, 72, 40, 74, 1073, 1071, 81, 1072, 1030, 1090, 73, 1040,
-    82, 1074, 1083, 1081, 50, 60, 84, 75, 91, 76, 1082, 90, 1100, 83, 1091, 92, 1084, 1050, 1060, 1075, 94, 100, 1076,
-    85, 1092, 1093, 101, 1120, 86, 1094, 1101, 77, 104, 1085, 1102, 102, 121, 1086, 1103, 1077, 95, 1104, 96, 93,
-    1095, 87, 1121, 1122, 120, 1110, 1096, 122, 1113, 105, 1087, 111, 1112, 103, 1114, 124, 1111, 1124, 1105, 110,
-    1130, 97, 1106, 131, 106, 130, 1131, 1097, 132, 113, 112, 114, 1125, 134, 1123, 1132, 125, 1134, 141, 1140, 1126,
-    107, 1107, 126, 123, 1166, 1135, 1142, 142, 1144, 140, 144, 1115, 1141, 115, 135, 1127, 127, 1143, 150, 1150, 170,
-    1152, 143, 152, 151, 167, 166, 1145, 154, 1151, 1146, 171, 146, 145, 1167, 1154, 153, 1153, 172, 1147, 156, 1156,
-    1155, 147, 155, 173, 157, 1157, 174,
+    0, 1000, 1070, 70, 20, 1020, 1010, 30, 1071, 71, 10, 72, 40, 80, 1030, 1072, 74, 1040, 1074, 1073, 1081, 1080, 81,
+    73, 50, 60, 75, 1084, 84, 1050, 90, 82, 1060, 1082, 1090, 1083, 1091, 1075, 91, 1076, 85, 94, 77, 1094, 83, 1100,
+    76, 1093, 1092, 1101, 100, 95, 101, 1085, 92, 1077, 1086, 104, 1104, 1102, 1103, 93, 86, 87, 1095, 105, 1121, 121,
+    102, 1087, 1096, 1120, 1122, 103, 124, 96, 111, 1124, 120, 1105, 1111, 110, 1112, 97, 1131, 125, 131, 1106, 1097,
+    122, 1132, 1110, 113, 106, 130, 1113, 1114, 1130, 1125, 1134, 112, 1126, 107, 132, 134, 114, 141, 115, 1107, 135,
+    1142, 123, 1123, 1140, 1141, 1135, 126, 1166, 140, 1115, 1144, 1146, 127, 1127, 151, 1152, 142, 144, 143, 1151,
+    1143, 145, 1150, 150, 1154, 170, 1145, 152, 171, 166, 154, 146, 153, 1156, 167, 1167, 1153, 172, 1147, 1155, 155,
+    147, 156, 173, 157, 1157, 174,
 )
 
 
@@ -260,13 +261,13 @@
         send(c, (HALVES, j), ref, ref, c.sum_plus)
         ref = c.rot.at[j, piece(c.q(1, 0)), hi]
         send(c, (HALVES, j), ref, ref, c.sum_minus)
-        if j in ASIDE:
+        if j in LATER:
             for d in (3, 1):
                 ref = c.rot.at[j, piece(c.q(d, 0))]
                 send(c, (DONE, SIDE, j), ref, ref, c.sum_partner)
 
     def across(c, j):
-        if j in ASIDE:
+        if j in LATER:
             arrived(c, (HALVES, j), c.rot.at[j, first])
             ref = c.rot.at[j, piece(c.q(2, 0))]
             send(c, (DONE, SIDE, j), ref, ref, c.sum_partner)
@@ -304,7 +305,7 @@
             for d in range(4):
                 share_rows(c, j, piece(c.q(d, 1)))
             return
-        if j in ASIDE:
+        if j in LATER:
             arrived(c, (DONE, SIDE, j), c.rot.at[j, pl.ds(0, 4 * PIECE)])
         else:
             arrived(c, (HALVES, j), c.rot.at[j, pl.ds(0, 2 * PIECE)])

time: 67.4 us -> 66.6 us (0.988)
  Pallas kernels: 66 us -> 65.2 us
    pallas_call x1, Pallas kernels: 66 us -> 65.2 us  [on_device(): pl.pallas_call(kernel, out_shape=(jax.ShapeDtypeStruct((NARROW, WIDE), F3...]
where the time goes in v6:
time: 66.6 us; the launch traced here: 66.5 us
  Pallas kernels  65.2 us (98%)
  local copies, waits for them, and re-layouts  1.32 us (2%)
    pallas_call x1, Pallas kernels, on_device(): pl.pallas_call(kernel, out_shape=(jax.ShapeDtypeStruct((NARROW, WIDE), F3...  65.2 us

profile of v6, /device:TPU:1, one launch (start us, length us, event | category | flops | bytes accessed | tf_op | source)
XLA Modules:
  0.0 66.5 jit_solution(15742593723129202984)
XLA Ops:
  0.0 65.2 %rotate_and_correlate.1 = (f32[512,1024]{1,0:T(8,128)S(1)}, bf16[8000,1024]{1,0:T(8,128)(2,1)}) custom-call(bf16[256,512]{1,0:T(8,128)(2,1)} %acts.1, bf16[128,1024]{1,0:T(8,128)(2,1)} %grads.1, bf16[512,1024]{1,0:T(8,128)(2,1)} %qa.1, bf16[1024,512]{1,0:T(8,128)(2,1)} %qs.1), custom_call_target="tpu_custom_call" | custom-call | flops 6442450944 | bytes 5242880 | tf_op jit(solution)/shard_map/rotate_and_correlate/pallas_call | solution.py:363
  65.2 1.3 %copy.6 = f32[512,1024]{1,0:T(8,128)} copy(f32[512,1024]{1,0:T(8,128)S(1)} %get-tuple-element.6) | data formatting | bytes 4194304

commit v7 on v6

--- a/solution.py
+++ b/solution.py
@@ -15,13 +15,14 @@
 WIDE = 1024
 NARROW = WIDE // 2
 TILE = 512
+LAST_TILE = 512
 DIRECT = (6, 7)
 ASIDE = (2, 3)
 LATER = (3,)
-ARRIVALS = 149
+ARRIVALS = 138
 SENT = 8000
 
-PASSES = ((-1, 0), (0, 2), (2, 4), (4, 6), (6, 7))
+PASSES = ((-1, 0), (0, 2), (2, 4), (4, 6))
 
 UP = 2.0 ** 30
 
@@ -31,9 +32,8 @@
     76, 1093, 1092, 1101, 100, 95, 101, 1085, 92, 1077, 1086, 104, 1104, 1102, 1103, 93, 86, 87, 1095, 105, 1121, 121,
     102, 1087, 1096, 1120, 1122, 103, 124, 96, 111, 1124, 120, 1105, 1111, 110, 1112, 97, 1131, 125, 131, 1106, 1097,
     122, 1132, 1110, 113, 106, 130, 1113, 1114, 1130, 1125, 1134, 112, 1126, 107, 132, 134, 114, 141, 115, 1107, 135,
-    1142, 123, 1123, 1140, 1141, 1135, 126, 1166, 140, 1115, 1144, 1146, 127, 1127, 151, 1152, 142, 144, 143, 1151,
-    1143, 145, 1150, 150, 1154, 170, 1145, 152, 171, 166, 154, 146, 153, 1156, 167, 1167, 1153, 172, 1147, 1155, 155,
-    147, 156, 173, 157, 1157, 174,
+    1142, 123, 1123, 1140, 1141, 1135, 126, 1166, 140, 1115, 1144, 1146, 127, 1127, 142, 144, 143, 1143, 145, 170,
+    1145, 171, 166, 146, 167, 1167, 172, 1147, 147, 173,
 )
 
 
@@ -289,10 +289,11 @@
         send(c, (HALVES, j), ref, ref, c.sum_minus)
 
     def share_rows(c, j, rows):
+        now = sum(j > upto for _, upto in PASSES)
         if c is a:
-            send(c, (SHARED, j), rot_a.at[j, rows], rot_ao.at[j, rows], other)
-        else:
-            send(c, (SHARED, j), rot_g.at[j, rows, hi], rot_go.at[j, rows], other)
+            send(g, (SHARED, now), rot_a.at[j, rows], rot_ao.at[j, rows], other)
+        else:
+            send(g, (SHARED, now), rot_g.at[j, rows, hi], rot_go.at[j, rows], other)
 
     def share_early(c, j):
         arrived(c, (DONE, j), c.rot.at[j, pl.ds(0, 3 * PIECE)])
@@ -311,8 +312,9 @@
             arrived(c, (HALVES, j), c.rot.at[j, pl.ds(0, 2 * PIECE)])
         share_rows(c, j, pl.ds(0, HALF))
 
-    def receive(c, j):
-        arrived(c, (SHARED, j), rot_ao.at[j] if c is a else rot_go.at[j])
+    def receive(now):
+        above, upto = (PASSES + ((SLOTS - 2, SLOTS - 1),))[now]
+        arrived(g, (SHARED, now), wa.at[pl.ds(0, (upto - above) * (HALF + HALF // 2))])
 
     def ring_slot(up):
         return up + (up // 2) * (1 - 2 * (up % 2))
@@ -336,7 +338,7 @@
                     rows, columns, (((0,), (0,)), ((), ())), preferred_element_type=F32)
 
     steps = (own, forward_up, forward_down, partner_lo, partner_hi, partner_forward_up, partner_forward_down,
-             multiply, sum_second, sum_partner, finish, spread, across, spread_across, share, receive, share_early)
+             multiply, sum_second, sum_partner, finish, spread, across, spread_across, share, None, share_early)
     for code in ORDER:
         c, step, j = (g, a)[code // 1000], code % 1000 // 10, code % 10
         if step < 7:
@@ -344,12 +346,29 @@
         elif step < len(steps):
             steps[step](c, j)
         else:
+            receive(j)
             correlate(*PASSES[j])
 
-    @pl.loop(0, NARROW // 64)
+    receive(len(PASSES))
+    last_a = (yh + 1) % 2 * 4 + (x + 2) % 4
+    last_g = (z + 2) % 4 * 2 + (yl + 1) % 2
+    distinct = jnp.where(last_a == last_g, 0.0, 1.0)
+    in_first_a = jnp.where(last_a < 4, 1.0, 0.0)
+    in_first_g = jnp.where(last_g < 4, distinct, 0.0)
+
+    @pl.loop(0, WIDE // LAST_TILE)
     def _(n):
-        rows = pl.ds(pl.multiple_of(n * 64, 64), 64)
-        out[rows] = (sums[0, rows] * sums[0, rows] + sums[1, rows] * sums[1, rows]) * (1.0 / TOKENS)
+        cols = pl.ds(pl.multiple_of(n * LAST_TILE, LAST_TILE), LAST_TILE)
+
+        def product(t):
+            rows = jnp.concatenate([rot_g[g_slot(t), :, lo], rot_go[g_slot(t)]], axis=0)
+            columns = jnp.concatenate([rot_a[a_slot(t), :, cols], rot_ao[a_slot(t), :, cols]], axis=0)
+            return lax.dot_general(rows, columns, (((0,), (0,)), ((), ())), preferred_element_type=F32)
+
+        for_a, for_g = product(last_a), product(last_g)
+        block0 = sums[0, :, cols] + for_a * in_first_a + for_g * in_first_g
+        block1 = sums[1, :, cols] + for_a * (1.0 - in_first_a) + for_g * (distinct - in_first_g)
+        out[:, cols] = (block0 * block0 + block1 * block1) * (1.0 / TOKENS)
 
     assert len(names) == ARRIVALS
     pltpu.make_async_copy(total, total, send_sem).wait()

time: 66.6 us -> 66.5 us (level)
  no operation moved by 1% of the time
where the time goes in v7:
time: 66.5 us; the launch traced here: 66.4 us
  Pallas kernels  65.1 us (98%)
  local copies, waits for them, and re-layouts  1.32 us (2%)
    pallas_call x1, Pallas kernels, on_device(): pl.pallas_call(kernel, out_shape=(jax.ShapeDtypeStruct((NARROW, WIDE), F3...  65.1 us

profile of v7, /device:TPU:1, one launch (start us, length us, event | category | flops | bytes accessed | tf_op | source)
XLA Modules:
  0.0 66.4 jit_solution(8800463510731217435)
XLA Ops:
  0.0 65.1 %rotate_and_correlate.1 = (f32[512,1024]{1,0:T(8,128)S(1)}, bf16[8000,1024]{1,0:T(8,128)(2,1)}) custom-call(bf16[256,512]{1,0:T(8,128)(2,1)} %acts.1, bf16[128,1024]{1,0:T(8,128)(2,1)} %grads.1, bf16[512,1024]{1,0:T(8,128)(2,1)} %qa.1, bf16[1024,512]{1,0:T(8,128)(2,1)} %qs.1), custom_call_target="tpu_custom_call" | custom-call | flops 6442450944 | bytes 5242880 | tf_op jit(solution)/shard_map/rotate_and_correlate/pallas_call | solution.py:382
  65.1 1.3 %copy.6 = f32[512,1024]{1,0:T(8,128)} copy(f32[512,1024]{1,0:T(8,128)S(1)} %get-tuple-element.6) | data formatting | bytes 4194304

commit v8 on v7

--- a/solution.py
+++ b/solution.py
@@ -17,23 +17,23 @@
 TILE = 512
 LAST_TILE = 512
 DIRECT = (6, 7)
-ASIDE = (2, 3)
-LATER = (3,)
+ASIDE = (1, 2)
+LATER = (2,)
 ARRIVALS = 138
 SENT = 8000
 
-PASSES = ((-1, 0), (0, 2), (2, 4), (4, 6))
+PASSES = ((-1, 0), (0, 1), (1, 4), (4, 6))
 
 UP = 2.0 ** 30
 
 ORDER = (
-    0, 1000, 1070, 70, 20, 1020, 1010, 30, 1071, 71, 10, 72, 40, 80, 1030, 1072, 74, 1040, 1074, 1073, 1081, 1080, 81,
-    73, 50, 60, 75, 1084, 84, 1050, 90, 82, 1060, 1082, 1090, 1083, 1091, 1075, 91, 1076, 85, 94, 77, 1094, 83, 1100,
-    76, 1093, 1092, 1101, 100, 95, 101, 1085, 92, 1077, 1086, 104, 1104, 1102, 1103, 93, 86, 87, 1095, 105, 1121, 121,
-    102, 1087, 1096, 1120, 1122, 103, 124, 96, 111, 1124, 120, 1105, 1111, 110, 1112, 97, 1131, 125, 131, 1106, 1097,
-    122, 1132, 1110, 113, 106, 130, 1113, 1114, 1130, 1125, 1134, 112, 1126, 107, 132, 134, 114, 141, 115, 1107, 135,
-    1142, 123, 1123, 1140, 1141, 1135, 126, 1166, 140, 1115, 1144, 1146, 127, 1127, 142, 144, 143, 1143, 145, 170,
-    1145, 171, 166, 146, 167, 1167, 172, 1147, 147, 173,
+    0, 1000, 70, 1070, 1010, 1020, 10, 20, 30, 40, 1071, 74, 72, 1030, 73, 1080, 71, 1040, 1074, 1073, 80, 1081, 60,
+    84, 75, 50, 1090, 83, 1072, 1060, 1050, 1084, 90, 1083, 1076, 94, 1075, 1091, 1100, 81, 85, 93, 76, 1094, 1082,
+    82, 1093, 77, 100, 1086, 104, 1120, 95, 1085, 1104, 1077, 1101, 91, 92, 1103, 86, 1092, 103, 1096, 1095, 105, 87,
+    1121, 101, 1124, 124, 102, 1087, 110, 96, 123, 120, 1123, 1105, 113, 1114, 1102, 1106, 111, 1110, 97, 1097, 1134,
+    121, 112, 106, 1111, 1130, 1113, 1112, 130, 134, 125, 1125, 1133, 1131, 131, 1126, 1115, 133, 107, 122, 1140,
+    1166, 114, 1107, 1122, 166, 140, 126, 1141, 135, 1135, 115, 143, 141, 1144, 127, 1143, 1146, 1127, 142, 167, 144,
+    1142, 170, 1145, 171, 146, 1167, 145, 172, 147, 1147, 173,
 )
 
 

time: 66.5 us -> 66.7 us (level)
  no operation moved by 1% of the time
where the time goes in v8:
time: 66.7 us; the launch traced here: 66.6 us
  Pallas kernels  65.2 us (98%)
  local copies, waits for them, and re-layouts  1.32 us (2%)
    pallas_call x1, Pallas kernels, on_device(): pl.pallas_call(kernel, out_shape=(jax.ShapeDtypeStruct((NARROW, WIDE), F3...  65.2 us

profile of v8, /device:TPU:1, one launch (start us, length us, event | category | flops | bytes accessed | tf_op | source)
XLA Modules:
  0.0 66.6 jit_solution(2765105575128899330)
XLA Ops:
  0.0 65.2 %rotate_and_correlate.1 = (f32[512,1024]{1,0:T(8,128)S(1)}, bf16[8000,1024]{1,0:T(8,128)(2,1)}) custom-call(bf16[256,512]{1,0:T(8,128)(2,1)} %acts.1, bf16[128,1024]{1,0:T(8,128)(2,1)} %grads.1, bf16[512,1024]{1,0:T(8,128)(2,1)} %qa.1, bf16[1024,512]{1,0:T(8,128)(2,1)} %qs.1), custom_call_target="tpu_custom_call" | custom-call | flops 6442450944 | bytes 5242880 | tf_op jit(solution)/shard_map/rotate_and_correlate/pallas_call | solution.py:382
  65.3 1.3 %copy.6 = f32[512,1024]{1,0:T(8,128)} copy(f32[512,1024]{1,0:T(8,128)S(1)} %get-tuple-element.6) | data formatting | bytes 4194304

commit v9 on v7

--- a/solution.py
+++ b/solution.py
@@ -17,23 +17,23 @@
 TILE = 512
 LAST_TILE = 512
 DIRECT = (6, 7)
-ASIDE = (2, 3)
+ASIDE = (0, 3)
 LATER = (3,)
-ARRIVALS = 138
+ARRIVALS = 139
 SENT = 8000
 
-PASSES = ((-1, 0), (0, 2), (2, 4), (4, 6))
+PASSES = ((-1, 0), (0, 1), (1, 2), (2, 4), (4, 6))
 
 UP = 2.0 ** 30
 
 ORDER = (
-    0, 1000, 1070, 70, 20, 1020, 1010, 30, 1071, 71, 10, 72, 40, 80, 1030, 1072, 74, 1040, 1074, 1073, 1081, 1080, 81,
-    73, 50, 60, 75, 1084, 84, 1050, 90, 82, 1060, 1082, 1090, 1083, 1091, 1075, 91, 1076, 85, 94, 77, 1094, 83, 1100,
-    76, 1093, 1092, 1101, 100, 95, 101, 1085, 92, 1077, 1086, 104, 1104, 1102, 1103, 93, 86, 87, 1095, 105, 1121, 121,
-    102, 1087, 1096, 1120, 1122, 103, 124, 96, 111, 1124, 120, 1105, 1111, 110, 1112, 97, 1131, 125, 131, 1106, 1097,
-    122, 1132, 1110, 113, 106, 130, 1113, 1114, 1130, 1125, 1134, 112, 1126, 107, 132, 134, 114, 141, 115, 1107, 135,
-    1142, 123, 1123, 1140, 1141, 1135, 126, 1166, 140, 1115, 1144, 1146, 127, 1127, 142, 144, 143, 1143, 145, 170,
-    1145, 171, 166, 146, 167, 1167, 172, 1147, 147, 173,
+    0, 1000, 1070, 30, 1020, 10, 20, 1010, 71, 1072, 40, 74, 70, 1030, 72, 1073, 1071, 1082, 1040, 1074, 60, 84, 50,
+    81, 73, 1081, 82, 80, 75, 76, 1092, 1084, 1080, 1060, 1075, 94, 91, 92, 1083, 1050, 1076, 1091, 1094, 83, 85,
+    1090, 90, 1102, 77, 104, 1085, 86, 101, 1093, 1101, 1086, 1104, 1100, 1077, 95, 93, 102, 1095, 1103, 100, 1096,
+    1122, 124, 1121, 1120, 96, 114, 87, 121, 103, 1087, 1105, 105, 1112, 1113, 1110, 122, 134, 120, 111, 97, 1124,
+    1106, 1130, 1097, 1111, 106, 131, 1114, 1125, 113, 125, 1123, 1131, 1132, 130, 110, 1134, 115, 1126, 132, 112,
+    1115, 107, 1107, 123, 144, 135, 126, 1141, 1135, 1142, 1140, 140, 141, 1143, 1144, 142, 1127, 127, 1166, 1146,
+    170, 143, 171, 145, 172, 1145, 166, 146, 1167, 167, 173, 1147, 147, 174,
 )
 
 

time: 66.5 us -> 66.5 us (level)
  no operation moved by 1% of the time
where the time goes in v9:
time: 66.5 us; the launch traced here: 66.4 us
  Pallas kernels  65 us (98%)
  local copies, waits for them, and re-layouts  1.32 us (2%)
    pallas_call x1, Pallas kernels, on_device(): pl.pallas_call(kernel, out_shape=(jax.ShapeDtypeStruct((NARROW, WIDE), F3...  65 us

profile of v9, /device:TPU:1, one launch (start us, length us, event | category | flops | bytes accessed | tf_op | source)
XLA Modules:
  0.0 66.4 jit_solution(4253621260457273692)
XLA Ops:
  0.0 65.0 %rotate_and_correlate.1 = (f32[512,1024]{1,0:T(8,128)S(1)}, bf16[8000,1024]{1,0:T(8,128)(2,1)}) custom-call(bf16[256,512]{1,0:T(8,128)(2,1)} %acts.1, bf16[128,1024]{1,0:T(8,128)(2,1)} %grads.1, bf16[512,1024]{1,0:T(8,128)(2,1)} %qa.1, bf16[1024,512]{1,0:T(8,128)(2,1)} %qs.1), custom_call_target="tpu_custom_call" | custom-call | flops 6442450944 | bytes 5242880 | tf_op jit(solution)/shard_map/rotate_and_correlate/pallas_call | solution.py:382
  65.0 1.3 %copy.6 = f32[512,1024]{1,0:T(8,128)} copy(f32[512,1024]{1,0:T(8,128)S(1)} %get-tuple-element.6) | data formatting | bytes 4194304
